TPU v7x, 32 devices: a whole 2x2x4 slice. The times are simulated.
32 devices in a mesh: grp: 2 (over y), ta: 8 (over z, x), au: 2 (over core).
Axes of the slice: x: 2, y: 2, z: 4, core: 2. Of those that a mesh axis runs over, the one named last changes fastest.
Arguments:
- readings: float32 [16, 8, 256], P('grp', 'au', 'ta'), parts along dimension 0, may hold values from -6 to 6
- present: int32 [16, 8, 256], P('grp', 'au', 'ta'), parts along dimension 0, may hold values 0 or 1
- cell_of: int32 [256], P('ta'), may hold values from 0 to 127, as said below
- noise_var: float32 [256], P('ta'), may hold values from 4 to 160
- kappa: float32 [128], replicated, may hold values from 0.05 to 0.25
- speed: float32 [128], replicated, may hold values from -0.2 to 0.2
- process_var: float32 [128], replicated, may hold values from 0.01 to 0.1
- prior_mean: float32 [256], P('grp'), parts along dimension 0, may hold values from -6 to 6
- prior_var: float32 [128], replicated, may hold values from 0.1 to 1
Outputs:
- filtered_mean: float32 [128, 128], P(('grp', 'ta', 'au')), parts along dimension 0
- smoothed_mean: float32 [128, 128], P(('grp', 'ta', 'au')), parts along dimension 0
- smoothed_var: float32 [128, 128], P(('grp', 'ta', 'au')), parts along dimension 0
There are 2 independent parts, one for each index of `grp`. A program takes and returns all parts, laid end to end along the dimension named above; an argument that names none is the same for every part. Nothing has to cross between parts.
Inputs may be any that keep to these rules, and one draw needn't show every extreme that they name: `cell_of`: each sensor observes one cell; several sensors may share a cell.
All inputs are finite; a program needn't handle non-finite values. No bound on the sum of `present` on one device may be relied on, other than what follows from the above.
Results may differ from a plain program's by a relative error of at most 0.0003.
Values sent between devices are 32-bit elements; how exact they have to be, the bound alone decides.
A program may use at most 128 MiB of HBM per device.

v0:
```python
import jax
import jax.numpy as jnp
from jax import lax
from jax.sharding import PartitionSpec as P

HIGHEST = lax.Precision.HIGHEST


def carried_in(part, axis, combine, identity, reverse):
    count = lax.axis_size(axis)
    place = lax.axis_index(axis)
    ahead = count - 1 - place if reverse else place
    gathered = jax.tree.map(lambda a: lax.all_gather(a, axis), part)
    state = jax.tree.map(lambda a, e: jnp.zeros_like(a) + jnp.asarray(e, a.dtype), part, identity)

    def one(step, state):
        source = count - 1 - step if reverse else step
        return combine(
            state, jax.tree.map(lambda a: lax.dynamic_index_in_dim(a, source, 0, False), gathered)
        )

    return lax.fori_loop(0, ahead, one, state)


def product(left, right):
    return jnp.matmul(left, right, precision=HIGHEST)


def symmetric(matrix):
    return 0.5 * (matrix + jnp.swapaxes(matrix, -1, -2))


def transition(kappa, speed):
    size_state = kappa.shape[0]
    row_ids = jnp.arange(size_state)[:, None]
    col_ids = jnp.arange(size_state)[None, :]
    ahead = (col_ids == (row_ids + 1) % size_state).astype(jnp.float32)
    behind = (col_ids == (row_ids - 1) % size_state).astype(jnp.float32)
    center = (col_ids == row_ids).astype(jnp.float32)
    return (
        center * (1.0 - 2.0 * kappa)[:, None]
        + ahead * (kappa - 0.5 * speed)[:, None]
        + behind * (kappa + 0.5 * speed)[:, None]
    )


def predict(mean, covariance, transition_mat, process_var):
    moved_mean = product(transition_mat, mean)
    moved_cov = symmetric(
        product(product(transition_mat, covariance), transition_mat.T)
    ) + jnp.diag(process_var)
    return (moved_mean, moved_cov)


def update(mean, covariance, lam_row, info_row):
    root_lam = jnp.sqrt(lam_row)
    unit_mat = jnp.eye(mean.shape[0], dtype=jnp.float32)
    inner_mat = unit_mat + root_lam[:, None] * covariance * root_lam[None, :]
    factor = jnp.linalg.cholesky(inner_mat)
    solved = jax.scipy.linalg.cho_solve((factor, True), root_lam[:, None] * covariance)
    new_cov = symmetric(covariance - product(covariance * root_lam[None, :], solved))
    new_mean = mean + product(new_cov, info_row - lam_row * mean)
    return (new_mean, new_cov)


def pick(condition, chosen, other):
    return tuple(
        (
            jnp.where(condition, first_item, second_item)
            for first_item, second_item in zip(chosen, other)
        )
    )


def filter_identity(size_state):
    unit_mat = jnp.eye(size_state, dtype=jnp.float32)
    zero_vec = jnp.zeros((size_state,), jnp.float32)
    zero_mat = jnp.zeros((size_state, size_state), jnp.float32)
    return (unit_mat, zero_vec, zero_mat, zero_vec, zero_mat, jnp.zeros((), jnp.float32))


def join_filter(early, late):
    map_early, off_early, spread_early, pull_early, curv_early, flag_early = early
    map_late, off_late, spread_late, pull_late, curv_late, flag_late = late
    size_state = off_early.shape[0]
    unit_mat = jnp.eye(size_state, dtype=jnp.float32)
    spread_used = jnp.where(flag_early > 0, spread_early, unit_mat)
    spread_curv = product(spread_used, curv_late)
    kernel_mat = symmetric(spread_used + product(spread_curv, spread_used))
    kernel_factor = jnp.linalg.cholesky(kernel_mat)
    right_cols = jnp.concatenate([product(spread_used, map_late.T), spread_curv], axis=1)
    solved_cols = jax.scipy.linalg.cho_solve((kernel_factor, True), right_cols)
    carried = solved_cols[:, :size_state].T
    curv_middle = symmetric(solved_cols[:, size_state:])
    residual = pull_late - product(curv_late, off_early)
    pulled = residual - product(curv_middle, product(spread_used, residual))
    map_new = product(carried, map_early)
    off_new = product(carried, off_early + product(spread_early, pull_late)) + off_late
    spread_new = symmetric(product(product(carried, spread_early), map_late.T)) + spread_late
    pull_new = product(pulled, map_early) + pull_early
    curv_new = symmetric(product(product(map_early.T, curv_middle), map_early)) + curv_early
    merged = (map_new, off_new, spread_new, pull_new, curv_new, jnp.maximum(flag_early, flag_late))
    kept = pick(flag_late <= 0, early, merged)
    return pick(flag_early <= 0, late, kept)


def smooth_identity(size_state):
    return (
        jnp.eye(size_state, dtype=jnp.float32),
        jnp.zeros((size_state,), jnp.float32),
        jnp.zeros((size_state, size_state), jnp.float32),
    )


def join_smooth(early, late):
    gain_early, off_early, spread_early = early
    gain_late, off_late, spread_late = late
    gain_new = product(gain_early, gain_late)
    off_new = product(gain_early, off_late) + off_early
    spread_new = symmetric(product(product(gain_early, spread_late), gain_early.T)) + spread_early
    return (gain_new, off_new, spread_new)


def flip_smooth(higher, lower):
    return join_smooth(lower, higher)


def solve_one(factor, right_side):
    return jax.scipy.linalg.cho_solve((factor, True), right_side)


def fold_sequence(joiner, elements):
    first_item = tuple((item[0] for item in elements))
    rest_items = tuple((item[1:] for item in elements))

    def fold_step(carry, item):
        return (joiner(carry, item), None)

    folded, _ = lax.scan(fold_step, first_item, rest_items)
    return folded


def local(readings, present, cell_of, noise_var, kappa, speed, process_var, prior_mean, prior_var):
    size_state = kappa.shape[0]
    steps_dev = readings.shape[1]
    transition_mat = transition(kappa, speed)
    weight = present.astype(jnp.float32) / noise_var
    weighted = weight * readings
    cells = lax.all_gather(cell_of, "ta", axis=0, tiled=True)
    weight_here, weighted_here = (
        lax.all_to_all(weight, "ta", split_axis=0, concat_axis=2, tiled=True),
        lax.all_to_all(weighted, "ta", split_axis=0, concat_axis=2, tiled=True),
    )
    weight_here = weight_here[0]
    weighted_here = weighted_here[0]
    one_hot = (cells[:, None] == jnp.arange(size_state)[None, :]).astype(jnp.float32)
    lam_rows = product(weight_here, one_hot)
    info_rows = product(weighted_here, one_hot)
    unit_mat = jnp.eye(size_state, dtype=jnp.float32)
    shrink = 1.0 / (1.0 / process_var + lam_rows)
    mappings = (shrink / process_var)[:, :, None] * transition_mat[None]
    offsets = shrink * info_rows
    spreads = shrink[:, :, None] * unit_mat[None]
    pulls = product(info_rows / (1.0 + process_var * lam_rows), transition_mat)
    damped = lam_rows / (1.0 + process_var * lam_rows)
    curvatures = product(transition_mat.T[None], damped[:, :, None] * transition_mat[None])
    actives = jnp.ones((steps_dev,), jnp.float32)
    summary = fold_sequence(join_filter, (mappings, offsets, spreads, pulls, curvatures, actives))
    map_sum, off_sum, spread_sum, pull_sum, curv_sum, flag_sum = summary
    identity_f = filter_identity(size_state)
    before = carried_in(
        (map_sum, off_sum, spread_sum, pull_sum, curv_sum, flag_sum),
        ("ta", "au"),
        join_filter,
        identity_f,
        False,
    )
    zero_vec = jnp.zeros((size_state,), jnp.float32)
    zero_mat = jnp.zeros((size_state, size_state), jnp.float32)
    prior_element = (
        zero_mat,
        prior_mean,
        jnp.diag(prior_var),
        zero_vec,
        zero_mat,
        jnp.ones((), jnp.float32),
    )
    start = join_filter(prior_element, before)

    def forward(carry, inputs):
        mean, covariance = carry
        mean, covariance = predict(mean, covariance, transition_mat, process_var)
        mean, covariance = update(mean, covariance, inputs[0], inputs[1])
        return ((mean, covariance), (mean, covariance))

    _, (means, covariances) = lax.scan(forward, (start[1], start[2]), (lam_rows, info_rows))
    moved = product(transition_mat[None], covariances)
    predicted = symmetric(product(moved, transition_mat.T[None])) + jnp.diag(process_var)[None]
    factors = jnp.linalg.cholesky(predicted)
    gains = jnp.swapaxes(jax.vmap(solve_one)(factors, moved), 1, 2)
    forward_means = product(means, transition_mat.T)
    smooth_offsets = means - product(gains, forward_means[:, :, None])[:, :, 0]
    smooth_spreads = symmetric(covariances - product(gains, moved))
    at_end = (lax.axis_index("ta") == lax.axis_size("ta") - 1) & (
        lax.axis_index("au") == lax.axis_size("au") - 1
    )
    final_row = at_end & (jnp.arange(steps_dev) == steps_dev - 1)
    gains = jnp.where(final_row[:, None, None], 0.0, gains)
    smooth_offsets = jnp.where(final_row[:, None], means, smooth_offsets)
    smooth_spreads = jnp.where(final_row[:, None, None], covariances, smooth_spreads)
    gain_sum, soff_sum, sspread_sum = fold_sequence(
        join_smooth, (gains, smooth_offsets, smooth_spreads)
    )
    identity_s = smooth_identity(size_state)
    after = carried_in(
        (gain_sum, soff_sum, sspread_sum), ("ta", "au"), flip_smooth, identity_s, True
    )

    def back_step(carry, item):
        mean_next, cov_next = carry
        gain_now, off_now, spread_now = item
        mean_now = product(gain_now, mean_next) + off_now
        cov_now = symmetric(product(product(gain_now, cov_next), gain_now.T)) + spread_now
        return ((mean_now, cov_now), (mean_now, jnp.diagonal(cov_now)))

    _, (smoothed, variances) = lax.scan(
        back_step, (after[1], after[2]), (gains, smooth_offsets, smooth_spreads), reverse=True
    )
    return (means, smoothed, variances)


def solution(mesh):
    placed = (
        P("grp", "au", "ta"),
        P("grp", "au", "ta"),
        P("ta"),
        P("ta"),
        P(),
        P(),
        P(),
        P("grp"),
        P(),
    )
    return jax.shard_map(
        local,
        mesh=mesh,
        in_specs=placed,
        out_specs=(
            P(("grp", "ta", "au"), None),
            P(("grp", "ta", "au"), None),
            P(("grp", "ta", "au"), None),
        ),
        check_vma=False,
    )
```

profile of v0, /device:TPU:0, one launch (start us, length us, event | category | flops | bytes accessed | tf_op | source)
XLA Modules:
  0.0 1108.9 jit_solution(7607419403356619531)
XLA Ops:
  28.5 11.7 %all-reduce = s32[256]{0:T(256)S(1)} all-reduce(s32[256]{0:T(256)S(1)} %dynamic-update-slice.4), channel_id=1, replica_groups=mesh['grp'=2,'ta'=8,'au'=2] {'ta'}, use_global_device_ids=true, to_apply=%add | all-reduce | flops 256 | bytes 2048
  46.4 82.8 %while.109 = (s32[]{:T(128)}, f32[128,128]{1,0:T(8,128)S(1)}, f32[128]{0:T(128)S(1)}, f32[128,128]{1,0:T(8,128)S(1)}, f32[128]{0:T(128)S(1)}, /*index=5*/f32[128...) while((s32[]{:T(128)}, f32[128,128]{1,0:T(8,128)S(1)}, ...), condition=%wide.region_3.7_spmd, body=%wide.region_0.6_spmd.sunk | while | flops 303809536 | bytes 5057770 | solution.py:139
  47.9 11.7 %custom-call.56 = f32[128,128]{1,0:T(8,128)S(1)} custom-call(f32[128,128]{1,0:T(8,128)S(1)} %fusion.535), custom_call_target="Cholesky" | custom-call | tf_op jit(solution)/shard_map/while/body/eval_jaxpr/jit(cholesky)/cholesky/custom-call.1 | solution.py:90
  60.9 9.8 custom-call.57
  75.5 11.7 %custom-call.56 = f32[128,128]{1,0:T(8,128)S(1)} custom-call(f32[128,128]{1,0:T(8,128)S(1)} %fusion.535), custom_call_target="Cholesky" | custom-call | tf_op jit(solution)/shard_map/while/body/eval_jaxpr/jit(cholesky)/cholesky/custom-call.1 | solution.py:90
  88.5 9.8 custom-call.57
  103.1 11.7 %custom-call.56 = f32[128,128]{1,0:T(8,128)S(1)} custom-call(f32[128,128]{1,0:T(8,128)S(1)} %fusion.535), custom_call_target="Cholesky" | custom-call | tf_op jit(solution)/shard_map/while/body/eval_jaxpr/jit(cholesky)/cholesky/custom-call.1 | solution.py:90
  116.1 9.8 custom-call.57
  133.5 29.8 %all-reduce.1 = f32[16]{0:T(128)S(1)} all-reduce(f32[16]{0:T(128)S(1)} %dynamic-update-slice.5), channel_id=1, replica_groups=mesh['grp'=2,'ta'=8,'au'=2] {'ta','au'}, use_global_device_ids=true, to_apply=%add.1 | all-reduce | flops 16 | bytes 128
  163.3 17.0 %all-gather.8 = f32[16,1,128]{2,1,0:T(1,128)S(1)} all-gather(f32[1,1,128]{2,1,0:T(1,128)S(1)} %bitcast.807), channel_id=4, replica_groups=mesh['grp'=2,'ta'=8,'au'=2] {'ta','au'}, dimensions={0}, use_global_device_ids=true | all-gather | bytes 8704 | tf_op jit(solution)/shard_map/all_gather | solution.py:13
  180.3 19.0 %all-gather.9 = f32[16,1,128]{2,1,0:T(1,128)S(1)} all-gather(f32[1,1,128]{2,1,0:T(1,128)S(1)} %bitcast.810), channel_id=5, replica_groups=mesh['grp'=2,'ta'=8,'au'=2] {'ta','au'}, dimensions={0}, use_global_device_ids=true | all-gather | bytes 8704 | tf_op jit(solution)/shard_map/all_gather | solution.py:13
  205.2 39.1 %all-gather.21.cloned.1.call-done = f32[2048,128]{1,0:T(8,128)} async-done(((f32[128,128]{1,0:T(8,128)}), f32[2048,128]{1,0:T(8,128)}) %all-gather.21.cloned.1.call-update) | async-done | bytes 1048592 | tf_op jit(solution)/shard_map/all_gather | solution.py:13
  252.3 11.7 %custom-call.46 = f32[128,128]{1,0:T(8,128)S(1)} custom-call(f32[128,128]{1,0:T(8,128)S(1)} %fusion.249), custom_call_target="Cholesky" | custom-call | tf_op jit(solution)/shard_map/jit(cholesky)/cholesky/custom-call.1 | solution.py:90
  277.6 102.0 %while.114 = (s32[]{:T(128)}, f32[128]{0:T(128)S(1)}, f32[128,128]{1,0:T(8,128)S(1)}, f32[4,128]{1,0:T(4,128)S(1)}, f32[4,128,128]{2,1,0:T(8,128)S(1)}, /*index=...) while((s32[]{:T(128)}, f32[128]{0:T(128)S(1)}, ...), condition=%wide.region_7.11_spmd.clone, body=%wide.region_6.10_spmd.clone.sunk | while | flops 127320576 | bytes 1986219 | solution.py:196
  279.1 11.7 %custom-call.61 = f32[128,128]{1,0:T(8,128)S(1)} custom-call(f32[128,128]{1,0:T(8,128)S(1)} %get-tuple-element.1247), custom_call_target="Cholesky" | custom-call | tf_op jit(solution)/shard_map/while/body/eval_jaxpr/jit(cholesky)/cholesky/custom-call.1 | solution.py:59
  304.6 11.7 %custom-call.61 = f32[128,128]{1,0:T(8,128)S(1)} custom-call(f32[128,128]{1,0:T(8,128)S(1)} %get-tuple-element.1247), custom_call_target="Cholesky" | custom-call | tf_op jit(solution)/shard_map/while/body/eval_jaxpr/jit(cholesky)/cholesky/custom-call.1 | solution.py:59
  330.1 11.7 %custom-call.61 = f32[128,128]{1,0:T(8,128)S(1)} custom-call(f32[128,128]{1,0:T(8,128)S(1)} %get-tuple-element.1247), custom_call_target="Cholesky" | custom-call | tf_op jit(solution)/shard_map/while/body/eval_jaxpr/jit(cholesky)/cholesky/custom-call.1 | solution.py:59
  355.5 11.7 %custom-call.61 = f32[128,128]{1,0:T(8,128)S(1)} custom-call(f32[128,128]{1,0:T(8,128)S(1)} %get-tuple-element.1247), custom_call_target="Cholesky" | custom-call | tf_op jit(solution)/shard_map/while/body/eval_jaxpr/jit(cholesky)/cholesky/custom-call.1 | solution.py:59
  381.0 47.1 %custom-call.27 = f32[4,128,128]{2,1,0:T(8,128)S(1)} custom-call(f32[4,128,128]{2,1,0:T(8,128)S(1)} %add_multiply_fusion), custom_call_target="Cholesky" | custom-call | tf_op jit(solution)/shard_map/jit(cholesky)/cholesky | solution.py:199
  428.4 39.3 %custom-call.28 = f32[4,1,128,128]{2,3,1,0:T(8,128)S(1)} custom-call(f32[4,1,128,128]{3,2,1,0:T(8,128)S(1)} %select_bitcast_fusion.1), custom_call_target="InvertDiagBlocksLowerTriangular" | custom-call | tf_op jit(solution)/shard_map/vmap(jit(_cho_solve))/triangular_solve | solution.py:129
  475.1 533.0 %all-gather.10 = f32[16,1,128]{2,1,0:T(1,128)S(1)} all-gather(f32[1,1,128]{2,1,0:T(1,128)S(1)} %bitcast.811), channel_id=8, replica_groups=mesh['grp'=2,'ta'=8,'au'=2] {'ta','au'}, dimensions={0}, use_global_device_ids=true | all-gather | bytes 8704 | tf_op jit(solution)/shard_map/all_gather | solution.py:13
  1008.1 19.7 %all-gather.23.cloned.1.call-done = f32[2048,128]{0,1:T(8,128)} async-done(((f32[128,128]{0,1:T(8,128)}), f32[2048,128]{0,1:T(8,128)}) %all-gather.23.cloned.1.call-update) | async-done | bytes 1048592 | tf_op jit(solution)/shard_map/all_gather | solution.py:13
  1029.3 37.9 %all-gather.25.cloned.1.call-done = f32[2048,128]{1,0:T(8,128)} async-done(((f32[128,128]{1,0:T(8,128)}), f32[2048,128]{1,0:T(8,128)}) %all-gather.25.cloned.1.call-update) | async-done | bytes 1048592 | tf_op jit(solution)/shard_map/all_gather | solution.py:13
  1067.2 25.6 %while.112 = (s32[]{:T(128)}, f32[128]{0:T(128)S(1)}, f32[128,128]{1,0:T(8,128)S(1)}, s32[]{:T(128)}, f32[16,128,128]{2,1,0:T(8,128)S(1)}, /*index=5*/f32[16,128...) while((s32[]{:T(128)}, f32[128]{0:T(128)S(1)}, ...), condition=%wide.region_13.17_spmd, body=%wide.region_12.16_spmd.sunk | while | flops 50577540 | bytes 855727 | solution.py:22
  (463 shorter events, 186.7 us)
Async XLA Ops:
  8.6 13.7 %all-to-all-start.1 = ((f32[8,1,128]{2,1,0:T(1,128)}), f32[8,1,128]{2,1,0:T(1,128)S(1)}, u32[]{:S(2)}, u32[]{:S(2)}) async-start(f32[8,1,128]{2,1,0:T(1,128)} %reshape.326), calls=%async_computation.1 | async-start | bytes 8192 | tf_op jit(solution)/shard_map/all_to_all | solution.py:152
  15.9 0.7 copy-start.13
  15.9 0.7 copy-start.14
  16.5 0.7 copy-start.7
  22.3 19.2 %all-to-all-start = ((f32[8,1,128]{2,1,0:T(1,128)}), f32[8,1,128]{2,1,0:T(1,128)S(1)}, u32[]{:S(2)}, u32[]{:S(2)}) async-start(f32[8,1,128]{2,1,0:T(1,128)} %reshape.324), calls=%async_computation | async-start | bytes 8192 | tf_op jit(solution)/shard_map/all_to_all | solution.py:151
  25.7 173.6 %all-gather.17.cloned.1.call-start = ((), (), s32[]{:S(2)}) async-start(), calls=%async_computation.2 | async-start | bytes 1114112 | tf_op jit(solution)/shard_map/all_gather | solution.py:13
  25.7 0.7 copy-start.17
  27.6 0.7 copy-start.15
  43.0 0.7 copy-start.1
  44.2 0.7 copy-start.2
  45.4 0.9 slice-start
  45.4 1.0 slice-start.1
  129.2 0.6 copy-start.4
  129.2 0.7 copy-start.3
  129.2 1.4 copy-start
  129.8 75.3 %all-gather.19.cloned.1.call-start = ((), (), s32[]{:S(2)}) async-start(), calls=%async_computation.3 | async-start | bytes 1114112 | tf_op jit(solution)/shard_map/all_gather | solution.py:13
  130.6 113.7 %all-gather.21.cloned.1.call-start = ((), (), s32[]{:S(2)}) async-start(), calls=%async_computation.4 | async-start | bytes 1114112 | tf_op jit(solution)/shard_map/all_gather | solution.py:13
  131.3 896.4 %all-gather.23.cloned.1.call-start = ((), (), s32[]{:S(2)}) async-start(), calls=%async_computation.5 | async-start | bytes 1114112 | tf_op jit(solution)/shard_map/all_gather | solution.py:13
  131.4 0.7 copy-start.16
  250.5 0.7 copy-start.8
  276.4 0.7 copy-start.12
  379.7 90.6 %copy-start.9 = (f32[4,128]{1,0:T(4,128)}, f32[4,128]{1,0:T(4,128)S(1)}, u32[]{:S(2)}) copy-start(f32[4,128]{1,0:T(4,128)S(1)} %get-tuple-element.596) | copy-start | bytes 6148
  473.9 0.7 copy-start.6
  474.5 592.7 %all-gather.25.cloned.1.call-start = ((), (), s32[]{:S(2)}) async-start(), calls=%async_computation.6 | async-start | bytes 1114112 | tf_op jit(solution)/shard_map/all_gather | solution.py:13
  (3 other events, 1.8 us)
Sparse Core Ops, SparseCore 0:
  130.0 36.0 all-gather.16
  168.2 36.8 all-gather.18
  207.3 36.8 all-gather.20
  474.6 553.0 all-gather.22
  1029.8 37.4 all-gather.24
where the time goes:
time: 1120 us; the launch traced here: 1110 us
  blocking collectives  611 us (55%)
  other arithmetic  287 us (26%)
  waiting for transfers between devices  109 us (10%)
  matrix products  42.6 us (4%)
  local copies, waits for them, and re-layouts  25.5 us (2%)
  between operations  15.3 us (1%)
    all_gather x3, blocking collectives, carried_in(): gathered = jax.tree.map(lambda a: lax.all_gather(a, axis), part)  569 us
    all_gather x5, waiting for transfers between devices, carried_in(): gathered = jax.tree.map(lambda a: lax.all_gather(a, axis), part)  103 us
    another operation x12, other arithmetic, join_filter(): kernel_factor = jnp.linalg.cholesky(kernel_mat)  49.6 us
    another operation x12, other arithmetic, update(): factor = jnp.linalg.cholesky(inner_mat)  49.6 us
    another operation x3, other arithmetic, local(): factors = jnp.linalg.cholesky(predicted)  47.3 us
    another operation x9, other arithmetic, join_filter(): solved_cols = jax.scipy.linalg.cho_solve((kernel_factor, True), right_cols)  41.9 us
    another operation x8, other arithmetic, update(): jax.scipy.linalg.cho_solve((factor, True), root_lam[:, None] * covariance)  41.9 us
    unnamed x2, blocking collectives  41.5 us
  transfers between devices with their start and end apart: 7, of which 5 were waited for; matrix products, arithmetic and copies ran while one was open for 1% of the time, Pallas kernels for 0%

commit v1 on v0

v1 whole, which is shorter than its diff:
```python
import functools

import jax
import jax.numpy as jnp
from jax import lax
from jax.experimental import pallas as pl
from jax.experimental.pallas import tpu as pltpu
from jax.sharding import PartitionSpec as P

HIGHEST = lax.Precision.HIGHEST
PANEL = 32


def mm(a, b):
    return lax.dot_general(
        a, b, (((1,), (0,)), ((), ())), precision=HIGHEST, preferred_element_type=jnp.float32
    )


def mm_nt(a, b):
    return lax.dot_general(
        a, b, (((1,), (1,)), ((), ())), precision=HIGHEST, preferred_element_type=jnp.float32
    )


def mm_tn(a, b):
    return lax.dot_general(
        a, b, (((0,), (0,)), ((), ())), precision=HIGHEST, preferred_element_type=jnp.float32
    )


def eye_mask(n):
    return lax.broadcasted_iota(jnp.int32, (n, n), 0) == lax.broadcasted_iota(
        jnp.int32, (n, n), 1
    )


def diag_of(row):
    n = row.shape[1]
    return jnp.where(eye_mask(n), jnp.broadcast_to(row, (n, n)), 0.0)


def sweep_panels(panels):
    lanes = lax.broadcasted_iota(jnp.int32, panels[0].shape, 1)
    subs = lax.broadcasted_iota(jnp.int32, panels[0].shape, 0)
    row_lanes = lax.broadcasted_iota(jnp.int32, (1, panels[0].shape[1]), 1)
    for j in range(PANEL):
        out = []
        for panel in panels:
            col = panel[:, j : j + 1]
            row = panel[j : j + 1, :]
            inv = 1.0 / panel[j : j + 1, j : j + 1]
            row = jnp.where(row_lanes == j, -1.0, row) * inv
            rest = jnp.where(lanes == j, 0.0, panel)
            out.append(jnp.where(subs == j, row, rest - col * row))
        panels = out
    return panels


def inverses(mats, work):
    n = mats[0].shape[0]
    count = len(mats)
    for i, mat in enumerate(mats):
        work[i] = mat

    def block(_, carry):
        rows = [work[i, :PANEL, :] for i in range(count)]
        swept = sweep_panels(rows)
        lanes = lax.broadcasted_iota(jnp.int32, (PANEL, n), 1)
        for i in range(count):
            cross = jnp.where(lanes < PANEL, 0.0, rows[i])
            low = work[i, PANEL:, :]
            low_lanes = lax.broadcasted_iota(jnp.int32, low.shape, 1)
            change = mm_tn(cross, swept[i])
            low = jnp.where(low_lanes < PANEL, 0.0, low) - change[PANEL:, :]
            work[i, : n - PANEL, :] = pltpu.roll(low, n - PANEL, 1)
            work[i, n - PANEL :, :] = pltpu.roll(swept[i], n - PANEL, 1)
        return carry

    lax.fori_loop(0, n // PANEL, block, 0)
    return [-work[i] for i in range(count)]


def middle(first, second):
    return first[2] + second[0]


def joined(first, second, inv):
    e1, g1, _, v1, w1 = first
    _, g2, h2, v2, w2 = second
    u = mm(w1 + v2, inv)
    left = mm(g1, inv)
    right = mm(inv, g2)
    return (
        e1 - mm_nt(left, g1),
        mm(left, g2),
        h2 - mm_tn(g2, right),
        v1 + mm_nt(u, g1),
        w2 + mm(u, g2),
    )


def joined_high(first, second, inv):
    _, g2, h2, v2, w2 = second
    u = mm(first[4] + v2, inv)
    return h2 - mm_tn(g2, mm(inv, g2)), w2 + mm(u, g2)


def joined_low(first, second, inv):
    e1, g1, _, v1, w1 = first
    u = mm(w1 + second[3], inv)
    return e1 - mm_nt(mm(g1, inv), g1), v1 + mm_nt(u, g1)


def put(ref, at, element):
    n = element[0].shape[0]
    ref[at, 0:n, :] = element[0]
    ref[at, n : 2 * n, :] = element[1]
    ref[at, 2 * n : 3 * n, :] = element[2]
    ref[at, 3 * n : 3 * n + 1, :] = element[3]
    ref[at, 3 * n + 1 : 3 * n + 2, :] = element[4]
    ref[at, 3 * n + 2 : 3 * n + 8, :] = jnp.zeros((6, n), jnp.float32)


def get(ref, at):
    n = ref.shape[2]
    return (
        ref[at, 0:n, :],
        ref[at, n : 2 * n, :],
        ref[at, 2 * n : 3 * n, :],
        ref[at, 3 * n : 3 * n + 1, :],
        ref[at, 3 * n + 1 : 3 * n + 2, :],
    )


def first_kernel(cov_ref, out_ref, work):
    out_ref[...] = inverses([cov_ref[...]], work)[0]


def local_kernel(place_ref, data_ref, trans_ref, g_ref, e_ref, q_ref, first_ref, prior_ref,
                 locals_ref, agg_ref, work):
    n = trans_ref.shape[0]
    steps = (data_ref.shape[0] - 1) // 2
    trans = trans_ref[...]
    pull = g_ref[...]
    curv = e_ref[...]
    var = q_ref[...]
    is_first = place_ref[0] == 0
    is_last = place_ref[0] == place_ref[1] - 1
    cells = data_ref[2 * steps : 2 * steps + 1, :]
    sensors = cells.shape[1]
    states = lax.broadcasted_iota(jnp.int32, (n, sensors), 0).astype(jnp.float32)
    one_hot = jnp.where(states == cells, 1.0, 0.0)
    sums = mm_nt(data_ref[0 : 2 * steps, :], one_hot)
    zero = jnp.zeros((n, n), jnp.float32)
    zero_row = jnp.zeros((1, n), jnp.float32)
    single = []
    for t in range(steps):
        lam, info = sums[t : t + 1, :], sums[steps + t : steps + t + 1, :]
        single.append((curv, pull, diag_of(1.0 / var + lam), zero_row, info))
    lam, info = sums[0:1, :], sums[steps : steps + 1, :]
    moved = mm_nt(prior_ref[...], trans)
    known = first_ref[...]
    head = (zero, zero, known + diag_of(lam), zero_row, info + mm(moved, known))
    single[0] = tuple(jnp.where(is_first, a, b) for a, b in zip(head, single[0]))
    lam, info = sums[steps - 1 : steps, :], sums[2 * steps - 1 : 2 * steps, :]
    damp = 1.0 / (1.0 + var * lam)
    tail = (
        mm_tn(trans, mm(diag_of(lam * damp), trans)), zero, zero,
        mm(info * damp, trans), zero_row,
    )
    tail = tuple(jnp.where(is_last, a, b) for a, b in zip(tail, single[3]))
    s0, s1, s2, s3 = single
    m01, m23, m23t = inverses([middle(s0, s1), middle(s2, s3), middle(s2, tail)], work)
    s01 = joined(s0, s1, m01)
    s23 = joined(s2, s3, m23)
    s23t = joined(s2, tail, m23t)
    put(locals_ref, 0, s0)
    put(locals_ref, 1, s01)
    put(locals_ref, 5, s23)
    put(locals_ref, 6, s3)
    pairs = [(s01, s2), (s01, s23), (s1, s23), (s01, s23t)]
    found = inverses([middle(a, b) for a, b in pairs], work)
    for slot, (a, b), inv in zip((2, 3, 4), pairs, found):
        put(locals_ref, slot, joined(a, b, inv))
    put(agg_ref, 0, joined(*pairs[3], found[3]))


def level_kernel(level, last, place_ref, own_ref, other_ref, sides_ref, agg_ref, out_ref, work):
    n = own_ref.shape[2]
    place = place_ref[0]
    span = 1 << level
    upper = (place // span) % 2 == 1
    inside = place % span
    own, other = get(own_ref, 0), get(other_ref, 0)

    def pick(a, b):
        return tuple(jnp.where(upper, x, y) for x, y in zip(a, b))

    wanted = []
    if not last:
        low, high = pick(other, own), pick(own, other)
        wanted.append(middle(low, high))
    if level > 0:
        before, after = get(sides_ref, 0), get(sides_ref, 1)
        alone = jnp.where(upper, inside == 0, inside == span - 1)
        one, two = pick(other, after), pick(before, other)
        unit = jnp.where(eye_mask(n), 1.0, 0.0)
        wanted.append(jnp.where(alone, unit, middle(one, two)))
    found = inverses(wanted, work)
    if not last:
        put(agg_ref, 0, joined(low, high, found[0]))
    if level > 0:
        merged = joined(one, two, found[-1])
        merged = tuple(jnp.where(alone, x, y) for x, y in zip(other, merged))
        put(out_ref, 0, pick(merged, before))
        put(out_ref, 1, pick(after, merged))
    else:
        empty = tuple(jnp.zeros_like(x) for x in other)
        put(out_ref, 0, pick(other, empty))
        put(out_ref, 1, pick(empty, other))


def final_kernel(place_ref, locals_ref, sides_ref, mean_ref, smooth_ref, var_ref, work):
    n = locals_ref.shape[2]
    is_first = place_ref[0] == 0
    unit = jnp.where(eye_mask(n), 1.0, 0.0)
    before = list(get(sides_ref, 0))
    before[2] = jnp.where(is_first, unit, before[2])
    after = get(sides_ref, 1)
    ahead = [get(locals_ref, i) for i in range(4)]
    behind = [get(locals_ref, i) for i in range(4, 7)]
    found = inverses(
        [middle(before, a) for a in ahead] + [middle(b, after) for b in behind], work
    )
    states = [joined_high(before, a, inv) for a, inv in zip(ahead, found[:4])]
    later = [joined_low(b, after, inv) for b, inv in zip(behind, found[4:])]
    later.append((after[0], after[3]))
    found = inverses(
        [s[0] for s in states] + [s[0] + l[0] for s, l in zip(states, later)], work
    )
    diagonal = eye_mask(n)
    for t in range(4):
        mean_ref[t : t + 1, :] = mm(states[t][1], found[t])
        smooth_ref[t : t + 1, :] = mm(states[t][1] + later[t][1], found[4 + t])
        var_ref[t : t + 1, :] = jnp.sum(
            jnp.where(diagonal, found[4 + t], 0.0), axis=0, keepdims=True
        )


def run(kernel, shapes, works, operands, n, scalars=1):
    specs = [pl.BlockSpec(memory_space=pltpu.SMEM)] * scalars
    specs += [pl.BlockSpec(memory_space=pltpu.VMEM)] * (len(operands) - scalars)
    single = not isinstance(shapes, list)
    outs = pl.BlockSpec(memory_space=pltpu.VMEM)
    return pl.pallas_call(
        kernel,
        out_shape=shapes,
        in_specs=specs,
        out_specs=outs if single else [outs] * len(shapes),
        scratch_shapes=[pltpu.VMEM((works, n, n), jnp.float32)],
        compiler_params=pltpu.CompilerParams(vmem_limit_bytes=40 * 2**20),
    )(*operands)


def transition(kappa, speed):
    n = kappa.shape[0]
    rows = jnp.arange(n)[:, None]
    cols = jnp.arange(n)[None, :]
    ahead = (cols == (rows + 1) % n).astype(jnp.float32)
    behind = (cols == (rows - 1) % n).astype(jnp.float32)
    center = (cols == rows).astype(jnp.float32)
    return (
        center * (1.0 - 2.0 * kappa)[:, None]
        + ahead * (kappa - 0.5 * speed)[:, None]
        + behind * (kappa + 0.5 * speed)[:, None]
    )


def local(readings, present, cell_of, noise_var, kappa, speed, process_var, prior_mean, prior_var):
    n = kappa.shape[0]
    outer, steps, sensors = readings.shape
    blocks = lax.axis_size("ta") * lax.axis_size("au")
    place = lax.axis_index("ta") * lax.axis_size("au") + lax.axis_index("au")
    where = jnp.stack([place, jnp.full_like(place, blocks)]).astype(jnp.int32)
    weight = present.astype(jnp.float32) / noise_var
    cells = jnp.broadcast_to(cell_of.astype(jnp.float32), (outer, 1, sensors))
    sent = jnp.concatenate([weight, weight * readings, cells], axis=1)
    data = lax.all_to_all(sent, "ta", split_axis=0, concat_axis=0, tiled=True)
    data = jnp.swapaxes(data, 0, 1).reshape(2 * steps + 1, outer * sensors)

    trans = transition(kappa, speed)
    pull = trans.T / process_var[None, :]
    curv = jnp.matmul(pull, trans, precision=HIGHEST)
    start = jnp.matmul(trans * prior_var[None, :], trans.T, precision=HIGHEST)
    start = start + jnp.diag(process_var)
    mat = jax.ShapeDtypeStruct((n, n), jnp.float32)
    known = run(first_kernel, mat, 1, [start], n, 0)

    def elements(count):
        return jax.ShapeDtypeStruct((count, 3 * n + 8, n), jnp.float32)

    pieces, agg = run(
        local_kernel, [elements(7), elements(1)], 4,
        [where, data, trans, pull, curv, process_var[None, :], known, prior_mean[None, :]], n,
    )
    sides = jnp.zeros((2, 3 * n + 8, n), jnp.float32)
    levels = blocks.bit_length() - 1
    for level in range(levels):
        pairs = [(i, i ^ (1 << level)) for i in range(blocks)]
        other = lax.ppermute(agg, ("ta", "au"), pairs)
        agg, sides = run(
            functools.partial(level_kernel, level, level == levels - 1),
            [elements(1), elements(2)], 2, [where, agg, other, sides], n,
        )
    row = jax.ShapeDtypeStruct((steps, n), jnp.float32)
    return tuple(run(final_kernel, [row, row, row], 8, [where, pieces, sides], n))


def solution(mesh):
    placed = (
        P("grp", "au", "ta"),
        P("grp", "au", "ta"),
        P("ta"),
        P("ta"),
        P(),
        P(),
        P(),
        P("grp"),
        P(),
    )
    out = P(("grp", "ta", "au"), None)
    return jax.shard_map(
        local, mesh=mesh, in_specs=placed, out_specs=(out, out, out), check_vma=False
    )
```

time: 1120 us -> 176 us (0.16)
  blocking collectives: 611 us -> 0 us
  other arithmetic: 287 us -> 3.7 us
  Pallas kernels: 0 us -> 134 us
  waiting for transfers between devices: 109 us -> 20 us
  matrix products: 42.6 us -> 2.09 us
  local copies, waits for them, and re-layouts: 25.5 us -> 1.41 us
  between operations: 15.3 us -> 0.74 us
    all_gather x3 -> x0, blocking collectives: 569 us -> none  [carried_in(): gathered = jax.tree.map(lambda a: lax.all_gather(a, axis), part)]
    another operation x46 -> x1, other arithmetic: 270 us -> 0.08 us  [local(): where = jnp.stack([place, jnp.full_like(place, blocks)]).astype(jnp.int32)]
    pallas_call x0 -> x7, Pallas kernels: none -> 134 us  [run(): pl.pallas_call(kernel, out_shape=shapes, in_specs=specs, out_specs=outs i...]
    all_gather x5 -> x0, waiting for transfers between devices: 103 us -> none  [carried_in(): gathered = jax.tree.map(lambda a: lax.all_gather(a, axis), part)]
    unnamed x2 -> x0, blocking collectives: 41.5 us -> none
    dot_general x147 -> x2, matrix products: 37.2 us -> 2.09 us  [the longest x1 1.1 us: local(): start = jnp.matmul(trans * prior_var[None, :], trans.T, precision=HIGHEST)]
    ppermute x0 -> x4, waiting for transfers between devices: none -> 20 us  [local(): other = lax.ppermute(agg, ('ta', 'au'), pairs)]
    add x23 -> x0, other arithmetic: 13.2 us -> none  [the longest x18 13 us: join_smooth(): symmetric(product(product(gain_early, spread_late), gain_early.T))]
  transfers between devices with their start and end apart: 7 -> 5, of which waited for: 5 -> 4; matrix products, arithmetic and copies ran while one was open for 1% -> 2% of each run, Pallas kernels for 0% -> 7%
where the time goes in v1:
time: 176 us; the launch traced here: 175 us
  Pallas kernels  134 us (76%)
  waiting for transfers between devices  20 us (11%)
  starting transfers between devices  13.5 us (8%)
  other arithmetic  3.7 us (2%)
  matrix products  2.09 us (1%)
    pallas_call x7, Pallas kernels, run(): pl.pallas_call(kernel, out_shape=shapes, in_specs=specs, out_specs=outs i...  134 us
    ppermute x4, waiting for transfers between devices, local(): other = lax.ppermute(agg, ('ta', 'au'), pairs)  20 us
    all_to_all x1, starting transfers between devices, local(): data = lax.all_to_all(sent, 'ta', split_axis=0, concat_axis=0, tiled=True)  7.25 us
    ppermute x4, starting transfers between devices, local(): other = lax.ppermute(agg, ('ta', 'au'), pairs)  6.22 us
  transfers between devices with their start and end apart: 5, of which 4 were waited for; matrix products, arithmetic and copies ran while one was open for 2% of the time, Pallas kernels for 7%

profile of v1, /device:TPU:0, one launch (start us, length us, event | category | flops | bytes accessed | tf_op | source)
XLA Modules:
  0.0 175.4 jit_solution(16253708915118323041)
XLA Ops:
  0.7 0.7 convert_element_type.10
  1.3 0.8 fusion.7
  2.1 0.7 reshape.61
  2.8 7.3 %all-to-all-start = ((f32[8,1,288]{2,1,0:T(1,128)}), f32[8,1,288]{2,1,0:T(1,128)S(1)}, u32[]{:S(2)}, u32[]{:S(2)}) async-start(f32[8,1,288]{2,1,0:T(1,128)} %reshape.61), calls=%async_computation | async-start | bytes 24576 | tf_op jit(solution)/shard_map/all_to_all | solution.py:289
  10.1 0.7 multiply_subtract_fusion.1
  10.8 1.0 fusion.2.e_ref
  11.8 0.8 add_divide_fusion
  12.6 1.1 convolution_add_fusion.cov_ref
  13.7 11.8 %shard_map.112.first_ref = f32[128,128]{1,0:T(8,128)S(1)} custom-call(f32[128,128]{1,0:T(8,128)S(1)} %convolution_add_fusion.cov_ref), custom_call_target="tpu_custom_call" | custom-call | tf_op jit(solution)/shard_map/pallas_call | solution.py:256
  25.6 0.5 broadcast.115
  26.1 0.7 reduce
  27.0 32.2 %shard_map.113 = (f32[7,392,128]{2,1,0:T(8,128)S(1)}, f32[1,392,128]{2,1,0:T(8,128)S(1)}) custom-call(s32[2]{0:T(128)S(1)} %pad_add_fusion.place_ref, f32[9,256]{1,0:T(8,128)S(1)} %reshape.60.data_ref, f32[128,128]{1,0:T(8,128)S(1)} %get-tuple-element.24.trans_ref, f32[128,128]{1,0:T(8,128)S(1)} %get-tuple-element.23.g_ref, f32[128,128]{1,0:T(8,128)S(1)} %fusion.2.e_ref, ...), custom_call_target="tpu_custom_call" | custom-call | tf_op jit(solution)/shard_map/pallas_call | solution.py:256
  59.1 1.5 collective-permute-done.other_ref
  60.6 13.1 %shard_map.114 = (f32[1,392,128]{2,1,0:T(8,128)S(1)}, f32[2,392,128]{2,1,0:T(8,128)S(1)}) custom-call(s32[2]{0:T(128)S(1)} %pad_add_fusion.place_ref, f32[1,392,128]{2,1,0:T(8,128)S(1)} %get-tuple-element.13.own_ref, f32[1,392,128]{2,1,0:T(8,128)S(1)} %collective-permute-done.other_ref, f32[2,392,128]{2,1,0:T(8,128)S(1)} %broadcast_in_dim.40.sides_ref), custom_call_target="tpu_custom_call" | custom-call | tf_op jit(solution)/shard_map/pallas_call | solution.py:256
  73.7 2.0 %collective-permute-start.1 = (f32[1,392,128]{2,1,0:T(8,128)S(1)}, f32[1,392,128]{2,1,0:T(8,128)S(1)}, u32[]{:S(2)}, u32[]{:S(2)}) collective-permute-start(f32[1,392,128]{2,1,0:T(8,128)S(1)} %get-tuple-element.14.own_ref), channel_id=1, source_target_pairs={{0,2},{1,3},{2,0},{3,1},{4,6},{5,7},{6,4},{7,5},{8,10},{9,11},{10,... | collective-permute-start | bytes 602120 | tf_op jit(solution)/shard_map/ppermute | solution.py:311
  75.8 5.3 %collective-permute-done.1.other_ref = f32[1,392,128]{2,1,0:T(8,128)S(1)} collective-permute-done((f32[1,392,128]{2,1,0:T(8,128)S(1)}, f32[1,392,128]{2,1,0:T(8,128)S(1)}, u32[]{:S(2)}, u32[]{:S(2)}) %collective-permute-start.1) | collective-permute-done | bytes 200736 | tf_op jit(solution)/shard_map/ppermute | solution.py:311
  81.1 14.0 %shard_map.115 = (f32[1,392,128]{2,1,0:T(8,128)S(1)}, f32[2,392,128]{2,1,0:T(8,128)S(1)}) custom-call(s32[2]{0:T(128)S(1)} %pad_add_fusion.place_ref, f32[1,392,128]{2,1,0:T(8,128)S(1)} %get-tuple-element.14.own_ref, f32[1,392,128]{2,1,0:T(8,128)S(1)} %collective-permute-done.1.other_ref, f32[2,392,128]{2,1,0:T(8,128)S(1)} %get-tuple-element.15.sides_ref), custom_call_target="tpu_custom_call" | custom-call | tf_op jit(solution)/shard_map/pallas_call | solution.py:256
  95.1 1.8 %collective-permute-start.2 = (f32[1,392,128]{2,1,0:T(8,128)S(1)}, f32[1,392,128]{2,1,0:T(8,128)S(1)}, u32[]{:S(2)}, u32[]{:S(2)}) collective-permute-start(f32[1,392,128]{2,1,0:T(8,128)S(1)} %get-tuple-element.16.own_ref), channel_id=1, source_target_pairs={{0,4},{1,5},{2,6},{3,7},{4,0},{5,1},{6,2},{7,3},{8,12},{9,13},{10,... | collective-permute-start | bytes 602120 | tf_op jit(solution)/shard_map/ppermute | solution.py:311
  96.9 4.8 %collective-permute-done.2.other_ref = f32[1,392,128]{2,1,0:T(8,128)S(1)} collective-permute-done((f32[1,392,128]{2,1,0:T(8,128)S(1)}, f32[1,392,128]{2,1,0:T(8,128)S(1)}, u32[]{:S(2)}, u32[]{:S(2)}) %collective-permute-start.2) | collective-permute-done | bytes 200736 | tf_op jit(solution)/shard_map/ppermute | solution.py:311
  101.6 14.2 %shard_map.116 = (f32[1,392,128]{2,1,0:T(8,128)S(1)}, f32[2,392,128]{2,1,0:T(8,128)S(1)}) custom-call(s32[2]{0:T(128)S(1)} %pad_add_fusion.place_ref, f32[1,392,128]{2,1,0:T(8,128)S(1)} %get-tuple-element.16.own_ref, f32[1,392,128]{2,1,0:T(8,128)S(1)} %collective-permute-done.2.other_ref, f32[2,392,128]{2,1,0:T(8,128)S(1)} %get-tuple-element.17.sides_ref), custom_call_target="tpu_custom_call" | custom-call | tf_op jit(solution)/shard_map/pallas_call | solution.py:256
  115.8 2.4 %collective-permute-start.3 = (f32[1,392,128]{2,1,0:T(8,128)S(1)}, f32[1,392,128]{2,1,0:T(8,128)S(1)}, u32[]{:S(2)}, u32[]{:S(2)}) collective-permute-start(f32[1,392,128]{2,1,0:T(8,128)S(1)} %get-tuple-element.18.own_ref), channel_id=1, source_target_pairs={{0,8},{1,9},{2,10},{3,11},{4,12},{5,13},{6,14},{7,15},{8,0},{9,1},... | collective-permute-start | bytes 602120 | tf_op jit(solution)/shard_map/ppermute | solution.py:311
  118.2 8.4 %collective-permute-done.3.other_ref = f32[1,392,128]{2,1,0:T(8,128)S(1)} collective-permute-done((f32[1,392,128]{2,1,0:T(8,128)S(1)}, f32[1,392,128]{2,1,0:T(8,128)S(1)}, u32[]{:S(2)}, u32[]{:S(2)}) %collective-permute-start.3) | collective-permute-done | bytes 200736 | tf_op jit(solution)/shard_map/ppermute | solution.py:311
  126.6 13.1 %shard_map.117 = (f32[1,392,128]{2,1,0:T(8,128)}, f32[2,392,128]{2,1,0:T(8,128)S(1)}) custom-call(s32[2]{0:T(128)S(1)} %pad_add_fusion.place_ref, f32[1,392,128]{2,1,0:T(8,128)S(1)} %get-tuple-element.18.own_ref, f32[1,392,128]{2,1,0:T(8,128)S(1)} %collective-permute-done.3.other_ref, f32[2,392,128]{2,1,0:T(8,128)S(1)} %get-tuple-element.19.sides_ref), custom_call_target="tpu_custom_call" | custom-call | tf_op jit(solution)/shard_map/pallas_call | solution.py:256
  139.7 35.7 %shard_map.118 = (f32[4,128]{1,0:T(4,128)}, f32[4,128]{1,0:T(4,128)}, f32[4,128]{1,0:T(4,128)}) custom-call(s32[2]{0:T(128)S(1)} %pad_add_fusion.place_ref, f32[7,392,128]{2,1,0:T(8,128)S(1)} %get-tuple-element.12.locals_ref, f32[2,392,128]{2,1,0:T(8,128)S(1)} %get-tuple-element.20.sides_ref), custom_call_target="tpu_custom_call" | custom-call | tf_op jit(solution)/shard_map/pallas_call | solution.py:256
  (14 shorter events, 0.3 us)
Async XLA Ops:
  0.6 26.3 %copy-start = (f32[128]{0:T(128)S(1)}, f32[128]{0:T(128)}, u32[]{:S(2)}) copy-start(f32[128]{0:T(128)} %param.15) | copy-start | bytes 1540
  0.6 26.3 %copy-start.1 = (f32[128]{0:T(128)S(1)}, f32[128]{0:T(128)}, u32[]{:S(2)}) copy-start(f32[128]{0:T(128)} %param.16) | copy-start | bytes 1540
  2.8 22.8 %all-to-all-start = ((f32[8,1,288]{2,1,0:T(1,128)}), f32[8,1,288]{2,1,0:T(1,128)S(1)}, u32[]{:S(2)}, u32[]{:S(2)}) async-start(f32[8,1,288]{2,1,0:T(1,128)} %reshape.61), calls=%async_computation | async-start | bytes 24576 | tf_op jit(solution)/shard_map/all_to_all | solution.py:289
  59.1 1.5 collective-permute-start
  73.7 7.3 %collective-permute-start.1 = (f32[1,392,128]{2,1,0:T(8,128)S(1)}, f32[1,392,128]{2,1,0:T(8,128)S(1)}, u32[]{:S(2)}, u32[]{:S(2)}) collective-permute-start(f32[1,392,128]{2,1,0:T(8,128)S(1)} %get-tuple-element.14.own_ref), channel_id=1, source_target_pairs={{0,2},{1,3},{2,0},{3,1},{4,6},{5,7},{6,4},{7,5},{8,10},{9,11},{10,... | collective-permute-start | bytes 602120 | tf_op jit(solution)/shard_map/ppermute | solution.py:311
  95.1 6.5 %collective-permute-start.2 = (f32[1,392,128]{2,1,0:T(8,128)S(1)}, f32[1,392,128]{2,1,0:T(8,128)S(1)}, u32[]{:S(2)}, u32[]{:S(2)}) collective-permute-start(f32[1,392,128]{2,1,0:T(8,128)S(1)} %get-tuple-element.16.own_ref), channel_id=1, source_target_pairs={{0,4},{1,5},{2,6},{3,7},{4,0},{5,1},{6,2},{7,3},{8,12},{9,13},{10,... | collective-permute-start | bytes 602120 | tf_op jit(solution)/shard_map/ppermute | solution.py:311
  115.8 10.8 %collective-permute-start.3 = (f32[1,392,128]{2,1,0:T(8,128)S(1)}, f32[1,392,128]{2,1,0:T(8,128)S(1)}, u32[]{:S(2)}, u32[]{:S(2)}) collective-permute-start(f32[1,392,128]{2,1,0:T(8,128)S(1)} %get-tuple-element.18.own_ref), channel_id=1, source_target_pairs={{0,8},{1,9},{2,10},{3,11},{4,12},{5,13},{6,14},{7,15},{8,0},{9,1},... | collective-permute-start | bytes 602120 | tf_op jit(solution)/shard_map/ppermute | solution.py:311

commit v2 on v1

--- a/solution.py
+++ b/solution.py
@@ -40,19 +40,44 @@
     return jnp.where(eye_mask(n), jnp.broadcast_to(row, (n, n)), 0.0)
 
 
+def four_rows(panel, j):
+    rows, n = panel.shape
+    row_lanes = lax.broadcasted_iota(jnp.int32, (1, n), 1)
+    cols = [jnp.broadcast_to(panel[:, j + m : j + m + 1], (rows, n)) for m in range(4)]
+    d = [[cols[m][j + i : j + i + 1, :] for m in range(4)] for i in range(4)]
+    r = []
+    for i in range(4):
+        row = jnp.where((row_lanes >= j) & (row_lanes < j + 4), 0.0, panel[j + i : j + i + 1, :])
+        r.append(jnp.where(row_lanes == j + i, -1.0, row))
+    inv = 1.0 / (d[0][0] * d[1][1] - d[1][0] * d[1][0])
+    a0, a1, a2 = d[1][1] * inv, d[1][0] * inv, d[0][0] * inv
+    x20, x21 = d[2][0] * a0 - d[2][1] * a1, d[2][1] * a2 - d[2][0] * a1
+    x30, x31 = d[3][0] * a0 - d[3][1] * a1, d[3][1] * a2 - d[3][0] * a1
+    s22 = d[2][2] - (x20 * d[2][0] + x21 * d[2][1])
+    s23 = d[3][2] - (x20 * d[3][0] + x21 * d[3][1])
+    s33 = d[3][3] - (x30 * d[3][0] + x31 * d[3][1])
+    inv = 1.0 / (s22 * s33 - s23 * s23)
+    y2 = r[2] - (x20 * r[0] + x21 * r[1])
+    y3 = r[3] - (x30 * r[0] + x31 * r[1])
+    w2 = inv * (s33 * y2 - s23 * y3)
+    w3 = inv * (s22 * y3 - s23 * y2)
+    w0 = (a0 * r[0] - a1 * r[1]) - (x20 * w2 + x30 * w3)
+    w1 = (a2 * r[1] - a1 * r[0]) - (x21 * w2 + x31 * w3)
+    return cols, [w0, w1, w2, w3]
+
+
 def sweep_panels(panels):
     lanes = lax.broadcasted_iota(jnp.int32, panels[0].shape, 1)
     subs = lax.broadcasted_iota(jnp.int32, panels[0].shape, 0)
-    row_lanes = lax.broadcasted_iota(jnp.int32, (1, panels[0].shape[1]), 1)
-    for j in range(PANEL):
+    for j in range(0, PANEL, 4):
+        found = [four_rows(panel, j) for panel in panels]
         out = []
-        for panel in panels:
-            col = panel[:, j : j + 1]
-            row = panel[j : j + 1, :]
-            inv = 1.0 / panel[j : j + 1, j : j + 1]
-            row = jnp.where(row_lanes == j, -1.0, row) * inv
-            rest = jnp.where(lanes == j, 0.0, panel)
-            out.append(jnp.where(subs == j, row, rest - col * row))
+        for panel, (cols, w) in zip(panels, found):
+            new = jnp.where((lanes >= j) & (lanes < j + 4), 0.0, panel)
+            new = new - ((cols[0] * w[0] + cols[1] * w[1]) + (cols[2] * w[2] + cols[3] * w[3]))
+            for m in range(4):
+                new = jnp.where(subs == j + m, w[m], new)
+            out.append(new)
         panels = out
     return panels
 
@@ -81,35 +106,47 @@
     return [-work[i] for i in range(count)]
 
 
-def middle(first, second):
-    return first[2] + second[0]
+def middle(spread, curv):
+    return spread + mm(mm(spread, curv), spread)
+
+
+def joined_with(first, second, left, mid, y):
+    e1, a1, _, p1, _ = first
+    e2, a2, c2, p2, b2 = second
+    return (
+        e1 + mm_tn(a1, mm(mm(e2, left), a1)),
+        mm(mm(a2, left), a1),
+        c2 + mm_nt(mm(a2, mid), a2),
+        p1 + mm(p2 - mm(y, e2), a1),
+        b2 + mm_nt(y, a2),
+    )
 
 
 def joined(first, second, inv):
-    e1, g1, _, v1, w1 = first
-    _, g2, h2, v2, w2 = second
-    u = mm(w1 + v2, inv)
-    left = mm(g1, inv)
-    right = mm(inv, g2)
-    return (
-        e1 - mm_nt(left, g1),
-        mm(left, g2),
-        h2 - mm_tn(g2, right),
-        v1 + mm_nt(u, g1),
-        w2 + mm(u, g2),
-    )
+    c1 = first[2]
+    left = mm(c1, inv)
+    y = mm_nt(first[4] + mm(second[3], c1), left)
+    return joined_with(first, second, left, mm(left, c1), y)
+
+
+def joined_step(first, info, scale, second, inv):
+    return joined_with(first, second, inv * scale, inv, mm(info + second[3], inv))
 
 
 def joined_high(first, second, inv):
-    _, g2, h2, v2, w2 = second
-    u = mm(first[4] + v2, inv)
-    return h2 - mm_tn(g2, mm(inv, g2)), w2 + mm(u, g2)
+    c1 = first[2]
+    _, a2, c2, p2, b2 = second
+    left = mm(c1, inv)
+    y = mm_nt(first[4] + mm(p2, c1), left)
+    return c2 + mm_nt(mm(a2, mm(left, c1)), a2), b2 + mm_nt(y, a2)
 
 
 def joined_low(first, second, inv):
-    e1, g1, _, v1, w1 = first
-    u = mm(w1 + second[3], inv)
-    return e1 - mm_nt(mm(g1, inv), g1), v1 + mm_nt(u, g1)
+    e1, a1, c1, p1, b1 = first
+    e2, p2 = second[0], second[3]
+    left = mm(c1, inv)
+    y = mm_nt(b1 + mm(p2, c1), left)
+    return e1 + mm_tn(a1, mm(mm(e2, left), a1)), p1 + mm(p2 - mm(y, e2), a1)
 
 
 def put(ref, at, element):
@@ -137,13 +174,11 @@
     out_ref[...] = inverses([cov_ref[...]], work)[0]
 
 
-def local_kernel(place_ref, data_ref, trans_ref, g_ref, e_ref, q_ref, first_ref, prior_ref,
+def local_kernel(place_ref, data_ref, trans_ref, q_ref, first_ref, prior_ref,
                  locals_ref, agg_ref, work):
     n = trans_ref.shape[0]
     steps = (data_ref.shape[0] - 1) // 2
     trans = trans_ref[...]
-    pull = g_ref[...]
-    curv = e_ref[...]
     var = q_ref[...]
     is_first = place_ref[0] == 0
     is_last = place_ref[0] == place_ref[1] - 1
@@ -154,39 +189,47 @@
     sums = mm_nt(data_ref[0 : 2 * steps, :], one_hot)
     zero = jnp.zeros((n, n), jnp.float32)
     zero_row = jnp.zeros((1, n), jnp.float32)
-    single = []
+    single, infos, scales = [], [], []
     for t in range(steps):
         lam, info = sums[t : t + 1, :], sums[steps + t : steps + t + 1, :]
-        single.append((curv, pull, diag_of(1.0 / var + lam), zero_row, info))
-    lam, info = sums[0:1, :], sums[steps : steps + 1, :]
+        damp = 1.0 / (1.0 + var * lam)
+        shrink = var * damp
+        single.append((
+            mm_tn(trans, mm(diag_of(lam * damp), trans)), mm(diag_of(damp), trans),
+            diag_of(shrink), mm(info * damp, trans), shrink * info,
+        ))
+        infos.append(info)
+        scales.append(1.0 / var + lam)
+    known = first_ref[...]
     moved = mm_nt(prior_ref[...], trans)
-    known = first_ref[...]
-    head = (zero, zero, known + diag_of(lam), zero_row, info + mm(moved, known))
-    single[0] = tuple(jnp.where(is_first, a, b) for a, b in zip(head, single[0]))
-    lam, info = sums[steps - 1 : steps, :], sums[2 * steps - 1 : 2 * steps, :]
-    damp = 1.0 / (1.0 + var * lam)
-    tail = (
-        mm_tn(trans, mm(diag_of(lam * damp), trans)), zero, zero,
-        mm(info * damp, trans), zero_row,
-    )
-    tail = tuple(jnp.where(is_last, a, b) for a, b in zip(tail, single[3]))
+    known_info = infos[0] + mm(moved, known)
+    info0 = jnp.where(is_first, known_info, infos[0])
+    high0 = jnp.where(is_first, known + diag_of(sums[0:1, :]), diag_of(scales[0]))
+    e3, _, _, p3, _ = single[3]
+    tail = tuple(
+        jnp.where(is_last, a, b) for a, b in zip((e3, zero, zero, p3, zero_row), single[3])
+    )
     s0, s1, s2, s3 = single
-    m01, m23, m23t = inverses([middle(s0, s1), middle(s2, s3), middle(s2, tail)], work)
-    s01 = joined(s0, s1, m01)
-    s23 = joined(s2, s3, m23)
-    s23t = joined(s2, tail, m23t)
+    m0, m01, m23 = inverses([high0, high0 + s1[0], diag_of(scales[2]) + s3[0]], work)
+    head = (zero, zero, m0, zero_row, mm(info0, m0))
+    s0 = tuple(jnp.where(is_first, a, b) for a, b in zip(head, s0))
+    s01 = joined_step(s0, info0, scales[0], s1, m01)
+    s23 = joined_step(s2, infos[2], scales[2], s3, m23)
+    s23t = joined_step(s2, infos[2], scales[2], tail, m23)
     put(locals_ref, 0, s0)
     put(locals_ref, 1, s01)
     put(locals_ref, 5, s23)
     put(locals_ref, 6, s3)
-    pairs = [(s01, s2), (s01, s23), (s1, s23), (s01, s23t)]
-    found = inverses([middle(a, b) for a, b in pairs], work)
-    for slot, (a, b), inv in zip((2, 3, 4), pairs, found):
-        put(locals_ref, slot, joined(a, b, inv))
-    put(agg_ref, 0, joined(*pairs[3], found[3]))
-
-
-def level_kernel(level, last, place_ref, own_ref, other_ref, sides_ref, agg_ref, out_ref, work):
+    found = inverses(
+        [middle(s01[2], s2[0]), middle(s01[2], s23[0]), diag_of(scales[1]) + s23[0]], work
+    )
+    put(locals_ref, 2, joined(s01, s2, found[0]))
+    put(locals_ref, 3, joined(s01, s23, found[1]))
+    put(locals_ref, 4, joined_step(s1, infos[1], scales[1], s23, found[2]))
+    put(agg_ref, 0, joined(s01, s23t, found[1]))
+
+
+def level_kernel(level, narrow, place_ref, own_ref, other_ref, sides_ref, agg_ref, out_ref, work):
     n = own_ref.shape[2]
     place = place_ref[0]
     span = 1 << level
@@ -197,19 +240,23 @@
     def pick(a, b):
         return tuple(jnp.where(upper, x, y) for x, y in zip(a, b))
 
-    wanted = []
-    if not last:
-        low, high = pick(other, own), pick(own, other)
-        wanted.append(middle(low, high))
+    low, high = pick(other, own), pick(own, other)
+    wanted = [middle(low[2], high[0])]
     if level > 0:
         before, after = get(sides_ref, 0), get(sides_ref, 1)
         alone = jnp.where(upper, inside == 0, inside == span - 1)
         one, two = pick(other, after), pick(before, other)
         unit = jnp.where(eye_mask(n), 1.0, 0.0)
-        wanted.append(jnp.where(alone, unit, middle(one, two)))
+        wanted.append(jnp.where(alone, unit, middle(one[2], two[0])))
     found = inverses(wanted, work)
-    if not last:
-        put(agg_ref, 0, joined(low, high, found[0]))
+    agg = joined(low, high, found[0])
+    if narrow:
+        above = (place // (2 * span)) % 2 == 1
+        agg_ref[0:n, :] = jnp.where(above, agg[0], agg[2])
+        agg_ref[n : n + 1, :] = jnp.where(above, agg[3], agg[4])
+        agg_ref[n + 1 : n + 8, :] = jnp.zeros((7, n), jnp.float32)
+    else:
+        put(agg_ref, 0, agg)
     if level > 0:
         merged = joined(one, two, found[-1])
         merged = tuple(jnp.where(alone, x, y) for x, y in zip(other, merged))
@@ -221,30 +268,54 @@
         put(out_ref, 1, pick(empty, other))
 
 
-def final_kernel(place_ref, locals_ref, sides_ref, mean_ref, smooth_ref, var_ref, work):
+def last_level(place, span, other_ref, sides_ref, work):
+    n = other_ref.shape[1]
+    upper = (place // span) % 2 == 1
+    inside = place % span
+    alone = jnp.where(upper, inside == 0, inside == span - 1)
+    before, after = get(sides_ref, 0), get(sides_ref, 1)
+    mat, vec = other_ref[0:n, :], other_ref[n : n + 1, :]
+    unit = jnp.where(eye_mask(n), 1.0, 0.0)
+    c1 = jnp.where(upper, mat, after[2])
+    e2 = jnp.where(upper, before[0], mat)
+    b1 = jnp.where(upper, vec, after[4])
+    p2 = jnp.where(upper, before[3], vec)
+    inv = inverses([jnp.where(alone, unit, middle(c1, e2))], work)[0]
+    left = mm(c1, inv)
+    y = mm_nt(b1 + mm(p2, c1), left)
+    link = jnp.where(upper, before[1].T, after[1])
+    core = jnp.where(upper, mm(left, c1), mm(e2, left))
+    y = jnp.where(upper, y, p2 - mm(y, e2))
+    new = jnp.where(upper, before[2], after[0]) + mm_tn(link, mm(core, link))
+    row = jnp.where(upper, before[4], after[3]) + mm(y, link)
+    new, row = jnp.where(alone, mat, new), jnp.where(alone, vec, row)
+    before = (None, None, jnp.where(upper, new, before[2]), None, jnp.where(upper, row, before[4]))
+    after = (jnp.where(upper, after[0], new), None, None, jnp.where(upper, after[3], row), None)
+    return before, after
+
+
+def final_kernel(span, place_ref, locals_ref, other_ref, sides_ref, mean_ref, smooth_ref, var_ref, work):
     n = locals_ref.shape[2]
     is_first = place_ref[0] == 0
     unit = jnp.where(eye_mask(n), 1.0, 0.0)
-    before = list(get(sides_ref, 0))
-    before[2] = jnp.where(is_first, unit, before[2])
-    after = get(sides_ref, 1)
+    before, after = last_level(place_ref[0], span, other_ref, sides_ref, work)
+    before = (None, None, jnp.where(is_first, unit, before[2]), None, before[4])
     ahead = [get(locals_ref, i) for i in range(4)]
     behind = [get(locals_ref, i) for i in range(4, 7)]
     found = inverses(
-        [middle(before, a) for a in ahead] + [middle(b, after) for b in behind], work
+        [middle(before[2], a[0]) for a in ahead] + [middle(b[2], after[0]) for b in behind], work
     )
     states = [joined_high(before, a, inv) for a, inv in zip(ahead, found[:4])]
     later = [joined_low(b, after, inv) for b, inv in zip(behind, found[4:])]
     later.append((after[0], after[3]))
-    found = inverses(
-        [s[0] for s in states] + [s[0] + l[0] for s, l in zip(states, later)], work
-    )
+    found = inverses([middle(s[0], l[0]) for s, l in zip(states, later)], work)
     diagonal = eye_mask(n)
-    for t in range(4):
-        mean_ref[t : t + 1, :] = mm(states[t][1], found[t])
-        smooth_ref[t : t + 1, :] = mm(states[t][1] + later[t][1], found[4 + t])
+    for t, ((cov, mean), (_, row)) in enumerate(zip(states, later)):
+        left = mm(cov, found[t])
+        mean_ref[t : t + 1, :] = mean
+        smooth_ref[t : t + 1, :] = mm_nt(mean + mm(row, cov), left)
         var_ref[t : t + 1, :] = jnp.sum(
-            jnp.where(diagonal, found[4 + t], 0.0), axis=0, keepdims=True
+            jnp.where(diagonal, mm(left, cov), 0.0), axis=0, keepdims=True
         )
 
 
@@ -290,8 +361,6 @@
     data = jnp.swapaxes(data, 0, 1).reshape(2 * steps + 1, outer * sensors)
 
     trans = transition(kappa, speed)
-    pull = trans.T / process_var[None, :]
-    curv = jnp.matmul(pull, trans, precision=HIGHEST)
     start = jnp.matmul(trans * prior_var[None, :], trans.T, precision=HIGHEST)
     start = start + jnp.diag(process_var)
     mat = jax.ShapeDtypeStruct((n, n), jnp.float32)
@@ -302,19 +371,28 @@
 
     pieces, agg = run(
         local_kernel, [elements(7), elements(1)], 4,
-        [where, data, trans, pull, curv, process_var[None, :], known, prior_mean[None, :]], n,
+        [where, data, trans, process_var[None, :], known, prior_mean[None, :]], n,
     )
     sides = jnp.zeros((2, 3 * n + 8, n), jnp.float32)
     levels = blocks.bit_length() - 1
     for level in range(levels):
         pairs = [(i, i ^ (1 << level)) for i in range(blocks)]
         other = lax.ppermute(agg, ("ta", "au"), pairs)
+        if level == levels - 1:
+            break
+        narrow = level == levels - 2
+        sent = jax.ShapeDtypeStruct((n + 8, n), jnp.float32) if narrow else elements(1)
         agg, sides = run(
-            functools.partial(level_kernel, level, level == levels - 1),
-            [elements(1), elements(2)], 2, [where, agg, other, sides], n,
+            functools.partial(level_kernel, level, narrow),
+            [sent, elements(2)], 2, [where, agg, other, sides], n,
         )
     row = jax.ShapeDtypeStruct((steps, n), jnp.float32)
-    return tuple(run(final_kernel, [row, row, row], 8, [where, pieces, sides], n))
+    return tuple(
+        run(
+            functools.partial(final_kernel, blocks // 2),
+            [row, row, row], 8, [where, pieces, other, sides], n,
+        )
+    )
 
 
 def solution(mesh):

time: 176 us -> 122 us (0.69)
  Pallas kernels: 134 us -> 87.2 us
  waiting for transfers between devices: 20 us -> 14.4 us
    pallas_call x7 -> x6, Pallas kernels: 134 us -> 87.2 us  [run(): pl.pallas_call(kernel, out_shape=shapes, in_specs=specs, out_specs=outs i...]
    ppermute x4, waiting for transfers between devices: 20 us -> 14.4 us  [local(): other = lax.ppermute(agg, ('ta', 'au'), pairs)]
  transfers between devices with their start and end apart: 5 -> 5, of which waited for: 4 -> 4; matrix products, arithmetic and copies ran while one was open for 2% -> 2% of each run, Pallas kernels for 7% -> 4%
where the time goes in v2:
time: 122 us; the launch traced here: 121 us
  Pallas kernels  87.2 us (71%)
  waiting for transfers between devices  14.4 us (12%)
  starting transfers between devices  13.5 us (11%)
  other arithmetic  3.04 us (2%)
  local copies, waits for them, and re-layouts  1.41 us (1%)
    pallas_call x6, Pallas kernels, run(): pl.pallas_call(kernel, out_shape=shapes, in_specs=specs, out_specs=outs i...  87.2 us
    ppermute x4, waiting for transfers between devices, local(): other = lax.ppermute(agg, ('ta', 'au'), pairs)  14.4 us
    all_to_all x1, starting transfers between devices, local(): data = lax.all_to_all(sent, 'ta', split_axis=0, concat_axis=0, tiled=True)  7.25 us
    ppermute x4, starting transfers between devices, local(): other = lax.ppermute(agg, ('ta', 'au'), pairs)  6.2 us
  transfers between devices with their start and end apart: 5, of which 4 were waited for; matrix products, arithmetic and copies ran while one was open for 2% of the time, Pallas kernels for 4%

profile of v2, /device:TPU:0, one launch (start us, length us, event | category | flops | bytes accessed | tf_op | source)
XLA Modules:
  0.0 121.3 jit_solution(17492619736145263055)
XLA Ops:
  0.7 0.7 convert_element_type.10
  1.3 0.8 fusion.5
  2.1 0.7 reshape.60
  2.8 7.3 %all-to-all-start = ((f32[8,1,288]{2,1,0:T(1,128)}), f32[8,1,288]{2,1,0:T(1,128)S(1)}, u32[]{:S(2)}, u32[]{:S(2)}) async-start(f32[8,1,288]{2,1,0:T(1,128)} %reshape.60), calls=%async_computation | async-start | bytes 24576 | tf_op jit(solution)/shard_map/all_to_all | solution.py:360
  10.1 0.7 multiply_subtract_fusion.1
  10.8 0.2 select_add_fusion.trans_ref
  10.9 1.1 convolution_add_fusion.cov_ref
  12.0 0.1 pad_add_fusion.place_ref
  12.1 5.2 %shard_map.112.first_ref = f32[128,128]{1,0:T(8,128)S(1)} custom-call(f32[128,128]{1,0:T(8,128)S(1)} %convolution_add_fusion.cov_ref), custom_call_target="tpu_custom_call" | custom-call | tf_op jit(solution)/shard_map/pallas_call | solution.py:327
  17.3 0.5 broadcast.101
  17.8 0.7 reduce
  18.6 0.1 reshape.59.data_ref
  18.7 22.2 %shard_map.113 = (f32[7,392,128]{2,1,0:T(8,128)S(1)}, f32[1,392,128]{2,1,0:T(8,128)S(1)}) custom-call(s32[2]{0:T(128)S(1)} %pad_add_fusion.place_ref, f32[9,256]{1,0:T(8,128)S(1)} %reshape.59.data_ref, f32[128,128]{1,0:T(8,128)S(1)} %select_add_fusion.trans_ref, f32[1,128]{1,0:T(1,128)S(1)} %bitcast.4, f32[128,128]{1,0:T(8,128)S(1)} %shard_map.112.first_ref, ...), custom_call_target="tpu_custom_call" | custom-call | tf_op jit(solution)/shard_map/pallas_call | solution.py:327
  40.9 1.4 %collective-permute-done.other_ref = f32[1,392,128]{2,1,0:T(8,128)S(1)} collective-permute-done((f32[1,392,128]{2,1,0:T(8,128)S(1)}, f32[1,392,128]{2,1,0:T(8,128)S(1)}, u32[]{:S(2)}, u32[]{:S(2)}) %collective-permute-start) | collective-permute-done | bytes 200736 | tf_op jit(solution)/shard_map/ppermute | solution.py:380
  42.4 7.8 %shard_map.114 = (f32[1,392,128]{2,1,0:T(8,128)S(1)}, f32[2,392,128]{2,1,0:T(8,128)S(1)}) custom-call(s32[2]{0:T(128)S(1)} %pad_add_fusion.place_ref, f32[1,392,128]{2,1,0:T(8,128)S(1)} %get-tuple-element.12.own_ref, f32[1,392,128]{2,1,0:T(8,128)S(1)} %collective-permute-done.other_ref, f32[2,392,128]{2,1,0:T(8,128)S(1)} %broadcast_in_dim.39.sides_ref), custom_call_target="tpu_custom_call" | custom-call | tf_op jit(solution)/shard_map/pallas_call | solution.py:327
  50.2 2.0 %collective-permute-start.1 = (f32[1,392,128]{2,1,0:T(8,128)S(1)}, f32[1,392,128]{2,1,0:T(8,128)S(1)}, u32[]{:S(2)}, u32[]{:S(2)}) collective-permute-start(f32[1,392,128]{2,1,0:T(8,128)S(1)} %get-tuple-element.13.own_ref), channel_id=1, source_target_pairs={{0,2},{1,3},{2,0},{3,1},{4,6},{5,7},{6,4},{7,5},{8,10},{9,11},{10,... | collective-permute-start | bytes 602120 | tf_op jit(solution)/shard_map/ppermute | solution.py:380
  52.2 5.3 %collective-permute-done.1.other_ref = f32[1,392,128]{2,1,0:T(8,128)S(1)} collective-permute-done((f32[1,392,128]{2,1,0:T(8,128)S(1)}, f32[1,392,128]{2,1,0:T(8,128)S(1)}, u32[]{:S(2)}, u32[]{:S(2)}) %collective-permute-start.1) | collective-permute-done | bytes 200736 | tf_op jit(solution)/shard_map/ppermute | solution.py:380
  57.5 9.5 %shard_map.115 = (f32[1,392,128]{2,1,0:T(8,128)S(1)}, f32[2,392,128]{2,1,0:T(8,128)S(1)}) custom-call(s32[2]{0:T(128)S(1)} %pad_add_fusion.place_ref, f32[1,392,128]{2,1,0:T(8,128)S(1)} %get-tuple-element.13.own_ref, f32[1,392,128]{2,1,0:T(8,128)S(1)} %collective-permute-done.1.other_ref, f32[2,392,128]{2,1,0:T(8,128)S(1)} %get-tuple-element.14.sides_ref), custom_call_target="tpu_custom_call" | custom-call | tf_op jit(solution)/shard_map/pallas_call | solution.py:327
  67.0 1.8 %collective-permute-start.2 = (f32[1,392,128]{2,1,0:T(8,128)S(1)}, f32[1,392,128]{2,1,0:T(8,128)S(1)}, u32[]{:S(2)}, u32[]{:S(2)}) collective-permute-start(f32[1,392,128]{2,1,0:T(8,128)S(1)} %get-tuple-element.15.own_ref), channel_id=1, source_target_pairs={{0,4},{1,5},{2,6},{3,7},{4,0},{5,1},{6,2},{7,3},{8,12},{9,13},{10,... | collective-permute-start | bytes 602120 | tf_op jit(solution)/shard_map/ppermute | solution.py:380
  68.7 4.8 %collective-permute-done.2.other_ref = f32[1,392,128]{2,1,0:T(8,128)S(1)} collective-permute-done((f32[1,392,128]{2,1,0:T(8,128)S(1)}, f32[1,392,128]{2,1,0:T(8,128)S(1)}, u32[]{:S(2)}, u32[]{:S(2)}) %collective-permute-start.2) | collective-permute-done | bytes 200736 | tf_op jit(solution)/shard_map/ppermute | solution.py:380
  73.5 9.4 %shard_map.116 = (f32[136,128]{1,0:T(8,128)S(1)}, f32[2,392,128]{2,1,0:T(8,128)S(1)}) custom-call(s32[2]{0:T(128)S(1)} %pad_add_fusion.place_ref, f32[1,392,128]{2,1,0:T(8,128)S(1)} %get-tuple-element.15.own_ref, f32[1,392,128]{2,1,0:T(8,128)S(1)} %collective-permute-done.2.other_ref, f32[2,392,128]{2,1,0:T(8,128)S(1)} %get-tuple-element.16.sides_ref), custom_call_target="tpu_custom_call" | custom-call | tf_op jit(solution)/shard_map/pallas_call | solution.py:327
  82.9 2.3 %collective-permute-start.3 = (f32[136,128]{1,0:T(8,128)S(1)}, f32[136,128]{1,0:T(8,128)S(1)}, u32[]{:S(2)}, u32[]{:S(2)}) collective-permute-start(f32[136,128]{1,0:T(8,128)S(1)} %get-tuple-element.17), channel_id=1, source_target_pairs={{0,8},{1,9},{2,10},{3,11},{4,12},{5,13},{6,14},{7,15},{8,0},{9,1},... | collective-permute-start | bytes 208904 | tf_op jit(solution)/shard_map/ppermute | solution.py:380
  85.2 2.9 %collective-permute-done.3.other_ref = f32[136,128]{1,0:T(8,128)S(1)} collective-permute-done((f32[136,128]{1,0:T(8,128)S(1)}, f32[136,128]{1,0:T(8,128)S(1)}, u32[]{:S(2)}, u32[]{:S(2)}) %collective-permute-start.3) | collective-permute-done | bytes 69664 | tf_op jit(solution)/shard_map/ppermute | solution.py:380
  88.1 33.1 %shard_map.117 = (f32[4,128]{1,0:T(4,128)}, f32[4,128]{1,0:T(4,128)}, f32[4,128]{1,0:T(4,128)}) custom-call(s32[2]{0:T(128)S(1)} %pad_add_fusion.place_ref, f32[7,392,128]{2,1,0:T(8,128)S(1)} %get-tuple-element.11.locals_ref, f32[136,128]{1,0:T(8,128)S(1)} %collective-permute-done.3.other_ref, f32[2,392,128]{2,1,0:T(8,128)S(1)} %get-tuple-element.18.sides_ref), custom_call_target="tpu_custom_call" | custom-call | tf_op jit(solution)/shard_map/pallas_call | solution.py:327
  (12 shorter events, 0.2 us)
Async XLA Ops:
  0.6 18.0 %copy-start = (f32[128]{0:T(128)S(1)}, f32[128]{0:T(128)}, u32[]{:S(2)}) copy-start(f32[128]{0:T(128)} %param.15) | copy-start | bytes 1540
  0.6 18.0 %copy-start.1 = (f32[128]{0:T(128)S(1)}, f32[128]{0:T(128)}, u32[]{:S(2)}) copy-start(f32[128]{0:T(128)} %param.16) | copy-start | bytes 1540
  2.8 14.5 %all-to-all-start = ((f32[8,1,288]{2,1,0:T(1,128)}), f32[8,1,288]{2,1,0:T(1,128)S(1)}, u32[]{:S(2)}, u32[]{:S(2)}) async-start(f32[8,1,288]{2,1,0:T(1,128)} %reshape.60), calls=%async_computation | async-start | bytes 24576 | tf_op jit(solution)/shard_map/all_to_all | solution.py:360
  40.8 1.5 %collective-permute-start = (f32[1,392,128]{2,1,0:T(8,128)S(1)}, f32[1,392,128]{2,1,0:T(8,128)S(1)}, u32[]{:S(2)}, u32[]{:S(2)}) collective-permute-start(f32[1,392,128]{2,1,0:T(8,128)S(1)} %get-tuple-element.12.own_ref), channel_id=1, source_target_pairs={{0,1},{1,0},{2,3},{3,2},{4,5},{5,4},{6,7},{7,6},{8,9},{9,8},{10,11... | collective-permute-start | bytes 602120 | tf_op jit(solution)/shard_map/ppermute | solution.py:380
  50.2 7.3 %collective-permute-start.1 = (f32[1,392,128]{2,1,0:T(8,128)S(1)}, f32[1,392,128]{2,1,0:T(8,128)S(1)}, u32[]{:S(2)}, u32[]{:S(2)}) collective-permute-start(f32[1,392,128]{2,1,0:T(8,128)S(1)} %get-tuple-element.13.own_ref), channel_id=1, source_target_pairs={{0,2},{1,3},{2,0},{3,1},{4,6},{5,7},{6,4},{7,5},{8,10},{9,11},{10,... | collective-permute-start | bytes 602120 | tf_op jit(solution)/shard_map/ppermute | solution.py:380
  67.0 6.5 %collective-permute-start.2 = (f32[1,392,128]{2,1,0:T(8,128)S(1)}, f32[1,392,128]{2,1,0:T(8,128)S(1)}, u32[]{:S(2)}, u32[]{:S(2)}) collective-permute-start(f32[1,392,128]{2,1,0:T(8,128)S(1)} %get-tuple-element.15.own_ref), channel_id=1, source_target_pairs={{0,4},{1,5},{2,6},{3,7},{4,0},{5,1},{6,2},{7,3},{8,12},{9,13},{10,... | collective-permute-start | bytes 602120 | tf_op jit(solution)/shard_map/ppermute | solution.py:380
  82.9 5.2 %collective-permute-start.3 = (f32[136,128]{1,0:T(8,128)S(1)}, f32[136,128]{1,0:T(8,128)S(1)}, u32[]{:S(2)}, u32[]{:S(2)}) collective-permute-start(f32[136,128]{1,0:T(8,128)S(1)} %get-tuple-element.17), channel_id=1, source_target_pairs={{0,8},{1,9},{2,10},{3,11},{4,12},{5,13},{6,14},{7,15},{8,0},{9,1},... | collective-permute-start | bytes 208904 | tf_op jit(solution)/shard_map/ppermute | solution.py:380

commit v3 on v2

--- a/solution.py
+++ b/solution.py
@@ -170,16 +170,22 @@
     )
 
 
-def first_kernel(cov_ref, out_ref, work):
-    out_ref[...] = inverses([cov_ref[...]], work)[0]
-
-
-def local_kernel(place_ref, data_ref, trans_ref, q_ref, first_ref, prior_ref,
-                 locals_ref, agg_ref, work):
-    n = trans_ref.shape[0]
+def transition(kappa, speed):
+    n = kappa.shape[1]
+    rows = lax.broadcasted_iota(jnp.int32, (n, n), 0)
+    cols = lax.broadcasted_iota(jnp.int32, (n, n), 1)
+    gap = jnp.where(rows < cols, rows - cols + n, rows - cols)
+    turned = jnp.where(gap == 0, 1.0 - 2.0 * kappa, 0.0)
+    turned = turned + jnp.where(gap == 1, kappa - 0.5 * speed, 0.0)
+    turned = turned + jnp.where(gap == n - 1, kappa + 0.5 * speed, 0.0)
+    return turned.T
+
+
+def local_kernel(place_ref, data_ref, param_ref, locals_ref, agg_ref, work):
+    n = param_ref.shape[1]
     steps = (data_ref.shape[0] - 1) // 2
-    trans = trans_ref[...]
-    var = q_ref[...]
+    trans = transition(param_ref[0:1, :], param_ref[1:2, :])
+    var = param_ref[2:3, :]
     is_first = place_ref[0] == 0
     is_last = place_ref[0] == place_ref[1] - 1
     cells = data_ref[2 * steps : 2 * steps + 1, :]
@@ -200,20 +206,28 @@
         ))
         infos.append(info)
         scales.append(1.0 / var + lam)
-    known = first_ref[...]
-    moved = mm_nt(prior_ref[...], trans)
-    known_info = infos[0] + mm(moved, known)
-    info0 = jnp.where(is_first, known_info, infos[0])
-    high0 = jnp.where(is_first, known + diag_of(sums[0:1, :]), diag_of(scales[0]))
+    moved_cov = mm_nt(trans * param_ref[4:5, :], trans)
+    cov0 = diag_of(var) + jnp.where(is_first, moved_cov, 0.0)
+    map0 = jnp.where(is_first, 0.0, trans)
+    mean0 = jnp.where(is_first, mm_nt(param_ref[3:4, :], trans), 0.0)
+    ahead0 = (zero, map0, cov0, zero_row, mean0)
+    lam0 = diag_of(sums[0:1, :])
     e3, _, _, p3, _ = single[3]
     tail = tuple(
         jnp.where(is_last, a, b) for a, b in zip((e3, zero, zero, p3, zero_row), single[3])
     )
-    s0, s1, s2, s3 = single
-    m0, m01, m23 = inverses([high0, high0 + s1[0], diag_of(scales[2]) + s3[0]], work)
-    head = (zero, zero, m0, zero_row, mm(info0, m0))
-    s0 = tuple(jnp.where(is_first, a, b) for a, b in zip(head, s0))
-    s01 = joined_step(s0, info0, scales[0], s1, m01)
+    _, s1, s2, s3 = single
+    seen = (lam0 + s1[0], s1[1], s1[2], infos[0] + s1[3], s1[4])
+    inv0, inv01, m23 = inverses(
+        [middle(cov0, lam0), middle(cov0, seen[0]), diag_of(scales[2]) + s3[0]], work
+    )
+    left = mm(cov0, inv0)
+    y = mm_nt(mean0 + mm(infos[0], cov0), left)
+    s0 = (
+        mm_tn(map0, mm(mm(lam0, left), map0)), mm(left, map0), mm(left, cov0),
+        mm(infos[0] - mm(y, lam0), map0), y,
+    )
+    s01 = joined(ahead0, seen, inv01)
     s23 = joined_step(s2, infos[2], scales[2], s3, m23)
     s23t = joined_step(s2, infos[2], scales[2], tail, m23)
     put(locals_ref, 0, s0)
@@ -334,20 +348,6 @@
     )(*operands)
 
 
-def transition(kappa, speed):
-    n = kappa.shape[0]
-    rows = jnp.arange(n)[:, None]
-    cols = jnp.arange(n)[None, :]
-    ahead = (cols == (rows + 1) % n).astype(jnp.float32)
-    behind = (cols == (rows - 1) % n).astype(jnp.float32)
-    center = (cols == rows).astype(jnp.float32)
-    return (
-        center * (1.0 - 2.0 * kappa)[:, None]
-        + ahead * (kappa - 0.5 * speed)[:, None]
-        + behind * (kappa + 0.5 * speed)[:, None]
-    )
-
-
 def local(readings, present, cell_of, noise_var, kappa, speed, process_var, prior_mean, prior_var):
     n = kappa.shape[0]
     outer, steps, sensors = readings.shape
@@ -360,18 +360,14 @@
     data = lax.all_to_all(sent, "ta", split_axis=0, concat_axis=0, tiled=True)
     data = jnp.swapaxes(data, 0, 1).reshape(2 * steps + 1, outer * sensors)
 
-    trans = transition(kappa, speed)
-    start = jnp.matmul(trans * prior_var[None, :], trans.T, precision=HIGHEST)
-    start = start + jnp.diag(process_var)
-    mat = jax.ShapeDtypeStruct((n, n), jnp.float32)
-    known = run(first_kernel, mat, 1, [start], n, 0)
+    params = jnp.stack([kappa, speed, process_var, prior_mean, prior_var])
 
     def elements(count):
         return jax.ShapeDtypeStruct((count, 3 * n + 8, n), jnp.float32)
 
     pieces, agg = run(
         local_kernel, [elements(7), elements(1)], 4,
-        [where, data, trans, process_var[None, :], known, prior_mean[None, :]], n,
+        [where, data, params], n,
     )
     sides = jnp.zeros((2, 3 * n + 8, n), jnp.float32)
     levels = blocks.bit_length() - 1

time: 122 us -> 122 us (level)
  waiting for transfers between devices: 14.4 us -> 24.7 us
  starting transfers between devices: 13.5 us -> 8.93 us
  Pallas kernels: 87.2 us -> 83.2 us
    all_to_all x1, waiting for transfers between devices: 0.01 us -> 5.74 us  [local(): data = lax.all_to_all(sent, 'ta', split_axis=0, concat_axis=0, tiled=True)]
    ppermute x4, waiting for transfers between devices: 14.4 us -> 19 us  [local(): other = lax.ppermute(agg, ('ta', 'au'), pairs)]
    ppermute x4, starting transfers between devices: 6.2 us -> 1.68 us  [local(): other = lax.ppermute(agg, ('ta', 'au'), pairs)]
    pallas_call x6 -> x5, Pallas kernels: 87.2 us -> 83.2 us  [run(): pl.pallas_call(kernel, out_shape=shapes, in_specs=specs, out_specs=outs i...]
  transfers between devices with their start and end apart: 5 -> 5, of which waited for: 4 -> 5; matrix products, arithmetic and copies ran while one was open for 2% -> 1% of each run, Pallas kernels for 4% -> 0%
where the time goes in v3:
time: 122 us
  Pallas kernels  83.2 us (68%)
  waiting for transfers between devices  24.7 us (20%)
  starting transfers between devices  8.93 us (7%)
  other arithmetic  2.19 us (2%)
  local copies, waits for them, and re-layouts  2.13 us (2%)
    pallas_call x5, Pallas kernels, run(): pl.pallas_call(kernel, out_shape=shapes, in_specs=specs, out_specs=outs i...  83.2 us
    ppermute x4, waiting for transfers between devices, local(): other = lax.ppermute(agg, ('ta', 'au'), pairs)  19 us
    all_to_all x1, starting transfers between devices, local(): data = lax.all_to_all(sent, 'ta', split_axis=0, concat_axis=0, tiled=True)  7.25 us
    all_to_all x1, waiting for transfers between devices, local(): data = lax.all_to_all(sent, 'ta', split_axis=0, concat_axis=0, tiled=True)  5.74 us
  transfers between devices with their start and end apart: 5, of which 5 were waited for; matrix products, arithmetic and copies ran while one was open for 1% of the time, Pallas kernels for 0%

profile of v3, /device:TPU:0, one launch (start us, length us, event | category | flops | bytes accessed | tf_op | source)
XLA Modules:
  0.0 121.9 jit_solution(14665296523752677362)
XLA Ops:
  0.6 0.7 convert_element_type.7
  1.3 0.8 fusion
  2.1 0.7 reshape.11
  2.8 7.3 %all-to-all-start = ((f32[8,1,288]{2,1,0:T(1,128)}), f32[8,1,288]{2,1,0:T(1,128)S(1)}, u32[]{:S(2)}, u32[]{:S(2)}) async-start(f32[8,1,288]{2,1,0:T(1,128)} %reshape.11), calls=%async_computation | async-start | bytes 24576 | tf_op jit(solution)/shard_map/all_to_all | solution.py:360
  10.0 0.1 pad_add_fusion.place_ref
  10.1 0.7 stack.31.param_ref
  10.8 5.7 %all-to-all-done = f32[8,1,288]{2,1,0:T(1,128)S(1)} async-done(((f32[8,1,288]{2,1,0:T(1,128)}), f32[8,1,288]{2,1,0:T(1,128)S(1)}, u32[]{:S(2)}, u32[]{:S(2)}) %all-to-all-start) | async-done | bytes 9248 | tf_op jit(solution)/shard_map/all_to_all | solution.py:360
  16.6 0.5 broadcast.1
  17.1 0.7 reduce
  17.8 0.1 reshape.12
  17.9 0.1 reshape.10.data_ref
  17.9 23.4 %shard_map.112 = (f32[7,392,128]{2,1,0:T(8,128)S(1)}, f32[1,392,128]{2,1,0:T(8,128)S(1)}) custom-call(s32[2]{0:T(128)S(1)} %pad_add_fusion.place_ref, f32[9,256]{1,0:T(8,128)S(1)} %reshape.10.data_ref, f32[5,128]{1,0:T(8,128)S(1)} %stack.31.param_ref), custom_call_target="tpu_custom_call" | custom-call | tf_op jit(solution)/shard_map/pallas_call | solution.py:341
  41.4 0.1 collective-permute-start
  41.4 1.4 %collective-permute-done.other_ref = f32[1,392,128]{2,1,0:T(8,128)S(1)} collective-permute-done((f32[1,392,128]{2,1,0:T(8,128)S(1)}, f32[1,392,128]{2,1,0:T(8,128)S(1)}, u32[]{:S(2)}, u32[]{:S(2)}) %collective-permute-start) | collective-permute-done | bytes 200736 | tf_op jit(solution)/shard_map/ppermute | solution.py:376
  42.9 7.8 %shard_map.113 = (f32[1,392,128]{2,1,0:T(8,128)S(1)}, f32[2,392,128]{2,1,0:T(8,128)S(1)}) custom-call(s32[2]{0:T(128)S(1)} %pad_add_fusion.place_ref, f32[1,392,128]{2,1,0:T(8,128)S(1)} %get-tuple-element.12.own_ref, f32[1,392,128]{2,1,0:T(8,128)S(1)} %collective-permute-done.other_ref, f32[2,392,128]{2,1,0:T(8,128)S(1)} %broadcast_in_dim.8.sides_ref), custom_call_target="tpu_custom_call" | custom-call | tf_op jit(solution)/shard_map/pallas_call | solution.py:341
  50.7 0.5 collective-permute-start.1
  51.2 6.5 %collective-permute-done.1.other_ref = f32[1,392,128]{2,1,0:T(8,128)S(1)} collective-permute-done((f32[1,392,128]{2,1,0:T(8,128)S(1)}, f32[1,392,128]{2,1,0:T(8,128)S(1)}, u32[]{:S(2)}, u32[]{:S(2)}) %collective-permute-start.1) | collective-permute-done | bytes 200736 | tf_op jit(solution)/shard_map/ppermute | solution.py:376
  57.7 9.5 %shard_map.114 = (f32[1,392,128]{2,1,0:T(8,128)S(1)}, f32[2,392,128]{2,1,0:T(8,128)S(1)}) custom-call(s32[2]{0:T(128)S(1)} %pad_add_fusion.place_ref, f32[1,392,128]{2,1,0:T(8,128)S(1)} %get-tuple-element.13.own_ref, f32[1,392,128]{2,1,0:T(8,128)S(1)} %collective-permute-done.1.other_ref, f32[2,392,128]{2,1,0:T(8,128)S(1)} %get-tuple-element.14.sides_ref), custom_call_target="tpu_custom_call" | custom-call | tf_op jit(solution)/shard_map/pallas_call | solution.py:341
  67.2 0.5 collective-permute-start.2
  67.7 5.7 %collective-permute-done.2.other_ref = f32[1,392,128]{2,1,0:T(8,128)S(1)} collective-permute-done((f32[1,392,128]{2,1,0:T(8,128)S(1)}, f32[1,392,128]{2,1,0:T(8,128)S(1)}, u32[]{:S(2)}, u32[]{:S(2)}) %collective-permute-start.2) | collective-permute-done | bytes 200736 | tf_op jit(solution)/shard_map/ppermute | solution.py:376
  73.4 9.4 %shard_map.115 = (f32[136,128]{1,0:T(8,128)S(1)}, f32[2,392,128]{2,1,0:T(8,128)S(1)}) custom-call(s32[2]{0:T(128)S(1)} %pad_add_fusion.place_ref, f32[1,392,128]{2,1,0:T(8,128)S(1)} %get-tuple-element.15.own_ref, f32[1,392,128]{2,1,0:T(8,128)S(1)} %collective-permute-done.2.other_ref, f32[2,392,128]{2,1,0:T(8,128)S(1)} %get-tuple-element.16.sides_ref), custom_call_target="tpu_custom_call" | custom-call | tf_op jit(solution)/shard_map/pallas_call | solution.py:341
  82.8 0.6 collective-permute-start.3
  83.4 5.3 %collective-permute-done.3.other_ref = f32[136,128]{1,0:T(8,128)S(1)} collective-permute-done((f32[136,128]{1,0:T(8,128)S(1)}, f32[136,128]{1,0:T(8,128)S(1)}, u32[]{:S(2)}, u32[]{:S(2)}) %collective-permute-start.3) | collective-permute-done | bytes 69664 | tf_op jit(solution)/shard_map/ppermute | solution.py:376
  88.7 33.1 %shard_map.116 = (f32[4,128]{1,0:T(4,128)}, f32[4,128]{1,0:T(4,128)}, f32[4,128]{1,0:T(4,128)}) custom-call(s32[2]{0:T(128)S(1)} %pad_add_fusion.place_ref, f32[7,392,128]{2,1,0:T(8,128)S(1)} %get-tuple-element.11.locals_ref, f32[136,128]{1,0:T(8,128)S(1)} %collective-permute-done.3.other_ref, f32[2,392,128]{2,1,0:T(8,128)S(1)} %get-tuple-element.18.sides_ref), custom_call_target="tpu_custom_call" | custom-call | tf_op jit(solution)/shard_map/pallas_call | solution.py:341
  (4 shorter events, 0.1 us)
Async XLA Ops:
  2.8 13.8 %all-to-all-start = ((f32[8,1,288]{2,1,0:T(1,128)}), f32[8,1,288]{2,1,0:T(1,128)S(1)}, u32[]{:S(2)}, u32[]{:S(2)}) async-start(f32[8,1,288]{2,1,0:T(1,128)} %reshape.11), calls=%async_computation | async-start | bytes 24576 | tf_op jit(solution)/shard_map/all_to_all | solution.py:360
  41.4 1.5 %collective-permute-start = (f32[1,392,128]{2,1,0:T(8,128)S(1)}, f32[1,392,128]{2,1,0:T(8,128)S(1)}, u32[]{:S(2)}, u32[]{:S(2)}) collective-permute-start(f32[1,392,128]{2,1,0:T(8,128)S(1)} %get-tuple-element.12.own_ref), channel_id=1, source_target_pairs={{0,1},{1,0},{2,3},{3,2},{4,5},{5,4},{6,7},{7,6},{8,9},{9,8},{10,11... | collective-permute-start | bytes 602120 | tf_op jit(solution)/shard_map/ppermute | solution.py:376
  50.7 7.0 %collective-permute-start.1 = (f32[1,392,128]{2,1,0:T(8,128)S(1)}, f32[1,392,128]{2,1,0:T(8,128)S(1)}, u32[]{:S(2)}, u32[]{:S(2)}) collective-permute-start(f32[1,392,128]{2,1,0:T(8,128)S(1)} %get-tuple-element.13.own_ref), channel_id=1, source_target_pairs={{0,2},{1,3},{2,0},{3,1},{4,6},{5,7},{6,4},{7,5},{8,10},{9,11},{10,... | collective-permute-start | bytes 602120 | tf_op jit(solution)/shard_map/ppermute | solution.py:376
  67.2 6.2 %collective-permute-start.2 = (f32[1,392,128]{2,1,0:T(8,128)S(1)}, f32[1,392,128]{2,1,0:T(8,128)S(1)}, u32[]{:S(2)}, u32[]{:S(2)}) collective-permute-start(f32[1,392,128]{2,1,0:T(8,128)S(1)} %get-tuple-element.15.own_ref), channel_id=1, source_target_pairs={{0,4},{1,5},{2,6},{3,7},{4,0},{5,1},{6,2},{7,3},{8,12},{9,13},{10,... | collective-permute-start | bytes 602120 | tf_op jit(solution)/shard_map/ppermute | solution.py:376
  82.8 5.9 %collective-permute-start.3 = (f32[136,128]{1,0:T(8,128)S(1)}, f32[136,128]{1,0:T(8,128)S(1)}, u32[]{:S(2)}, u32[]{:S(2)}) collective-permute-start(f32[136,128]{1,0:T(8,128)S(1)} %get-tuple-element.17), channel_id=1, source_target_pairs={{0,8},{1,9},{2,10},{3,11},{4,12},{5,13},{6,14},{7,15},{8,0},{9,1},... | collective-permute-start | bytes 208904 | tf_op jit(solution)/shard_map/ppermute | solution.py:376

commit v4 on v2

--- a/solution.py
+++ b/solution.py
@@ -309,14 +309,11 @@
     later = [joined_low(b, after, inv) for b, inv in zip(behind, found[4:])]
     later.append((after[0], after[3]))
     found = inverses([middle(s[0], l[0]) for s, l in zip(states, later)], work)
-    diagonal = eye_mask(n)
     for t, ((cov, mean), (_, row)) in enumerate(zip(states, later)):
-        left = mm(cov, found[t])
+        turned = mm(found[t], cov)
         mean_ref[t : t + 1, :] = mean
-        smooth_ref[t : t + 1, :] = mm_nt(mean + mm(row, cov), left)
-        var_ref[t : t + 1, :] = jnp.sum(
-            jnp.where(diagonal, mm(left, cov), 0.0), axis=0, keepdims=True
-        )
+        smooth_ref[t : t + 1, :] = mm(mean + mm(row, cov), turned)
+        var_ref[t : t + 1, :] = jnp.sum(turned * cov, axis=0, keepdims=True)
 
 
 def run(kernel, shapes, works, operands, n, scalars=1):

time: 122 us -> 121 us (level)
  no operation moved by 1% of the time
where the time goes in v4:
time: 121 us
  Pallas kernels  86.8 us (72%)
  waiting for transfers between devices  14.4 us (12%)
  starting transfers between devices  13.5 us (11%)
  other arithmetic  3.04 us (3%)
  local copies, waits for them, and re-layouts  1.41 us (1%)
    pallas_call x6, Pallas kernels, run(): pl.pallas_call(kernel, out_shape=shapes, in_specs=specs, out_specs=outs i...  86.8 us
    ppermute x4, waiting for transfers between devices, local(): other = lax.ppermute(agg, ('ta', 'au'), pairs)  14.4 us
    all_to_all x1, starting transfers between devices, local(): data = lax.all_to_all(sent, 'ta', split_axis=0, concat_axis=0, tiled=True)  7.25 us
    ppermute x4, starting transfers between devices, local(): other = lax.ppermute(agg, ('ta', 'au'), pairs)  6.2 us
  transfers between devices with their start and end apart: 5, of which 4 were waited for; matrix products, arithmetic and copies ran while one was open for 2% of the time, Pallas kernels for 4%

profile of v4, /device:TPU:0, one launch (start us, length us, event | category | flops | bytes accessed | tf_op | source)
XLA Modules:
  0.0 120.9 jit_solution(14028661684668097709)
XLA Ops:
  0.7 0.7 convert_element_type.10
  1.3 0.8 fusion.5
  2.1 0.7 reshape.60
  2.8 7.3 %all-to-all-start = ((f32[8,1,288]{2,1,0:T(1,128)}), f32[8,1,288]{2,1,0:T(1,128)S(1)}, u32[]{:S(2)}, u32[]{:S(2)}) async-start(f32[8,1,288]{2,1,0:T(1,128)} %reshape.60), calls=%async_computation | async-start | bytes 24576 | tf_op jit(solution)/shard_map/all_to_all | solution.py:357
  10.1 0.7 multiply_subtract_fusion.1
  10.8 0.2 select_add_fusion.trans_ref
  10.9 1.1 convolution_add_fusion.cov_ref
  12.0 0.1 pad_add_fusion.place_ref
  12.1 5.2 %shard_map.112.first_ref = f32[128,128]{1,0:T(8,128)S(1)} custom-call(f32[128,128]{1,0:T(8,128)S(1)} %convolution_add_fusion.cov_ref), custom_call_target="tpu_custom_call" | custom-call | tf_op jit(solution)/shard_map/pallas_call | solution.py:324
  17.3 0.5 broadcast.101
  17.8 0.7 reduce
  18.6 0.1 reshape.59.data_ref
  18.7 22.2 %shard_map.113 = (f32[7,392,128]{2,1,0:T(8,128)S(1)}, f32[1,392,128]{2,1,0:T(8,128)S(1)}) custom-call(s32[2]{0:T(128)S(1)} %pad_add_fusion.place_ref, f32[9,256]{1,0:T(8,128)S(1)} %reshape.59.data_ref, f32[128,128]{1,0:T(8,128)S(1)} %select_add_fusion.trans_ref, f32[1,128]{1,0:T(1,128)S(1)} %bitcast.4, f32[128,128]{1,0:T(8,128)S(1)} %shard_map.112.first_ref, ...), custom_call_target="tpu_custom_call" | custom-call | tf_op jit(solution)/shard_map/pallas_call | solution.py:324
  40.9 1.4 %collective-permute-done.other_ref = f32[1,392,128]{2,1,0:T(8,128)S(1)} collective-permute-done((f32[1,392,128]{2,1,0:T(8,128)S(1)}, f32[1,392,128]{2,1,0:T(8,128)S(1)}, u32[]{:S(2)}, u32[]{:S(2)}) %collective-permute-start) | collective-permute-done | bytes 200736 | tf_op jit(solution)/shard_map/ppermute | solution.py:377
  42.4 7.8 %shard_map.114 = (f32[1,392,128]{2,1,0:T(8,128)S(1)}, f32[2,392,128]{2,1,0:T(8,128)S(1)}) custom-call(s32[2]{0:T(128)S(1)} %pad_add_fusion.place_ref, f32[1,392,128]{2,1,0:T(8,128)S(1)} %get-tuple-element.12.own_ref, f32[1,392,128]{2,1,0:T(8,128)S(1)} %collective-permute-done.other_ref, f32[2,392,128]{2,1,0:T(8,128)S(1)} %broadcast_in_dim.39.sides_ref), custom_call_target="tpu_custom_call" | custom-call | tf_op jit(solution)/shard_map/pallas_call | solution.py:324
  50.2 2.0 %collective-permute-start.1 = (f32[1,392,128]{2,1,0:T(8,128)S(1)}, f32[1,392,128]{2,1,0:T(8,128)S(1)}, u32[]{:S(2)}, u32[]{:S(2)}) collective-permute-start(f32[1,392,128]{2,1,0:T(8,128)S(1)} %get-tuple-element.13.own_ref), channel_id=1, source_target_pairs={{0,2},{1,3},{2,0},{3,1},{4,6},{5,7},{6,4},{7,5},{8,10},{9,11},{10,... | collective-permute-start | bytes 602120 | tf_op jit(solution)/shard_map/ppermute | solution.py:377
  52.2 5.3 %collective-permute-done.1.other_ref = f32[1,392,128]{2,1,0:T(8,128)S(1)} collective-permute-done((f32[1,392,128]{2,1,0:T(8,128)S(1)}, f32[1,392,128]{2,1,0:T(8,128)S(1)}, u32[]{:S(2)}, u32[]{:S(2)}) %collective-permute-start.1) | collective-permute-done | bytes 200736 | tf_op jit(solution)/shard_map/ppermute | solution.py:377
  57.5 9.5 %shard_map.115 = (f32[1,392,128]{2,1,0:T(8,128)S(1)}, f32[2,392,128]{2,1,0:T(8,128)S(1)}) custom-call(s32[2]{0:T(128)S(1)} %pad_add_fusion.place_ref, f32[1,392,128]{2,1,0:T(8,128)S(1)} %get-tuple-element.13.own_ref, f32[1,392,128]{2,1,0:T(8,128)S(1)} %collective-permute-done.1.other_ref, f32[2,392,128]{2,1,0:T(8,128)S(1)} %get-tuple-element.14.sides_ref), custom_call_target="tpu_custom_call" | custom-call | tf_op jit(solution)/shard_map/pallas_call | solution.py:324
  67.0 1.8 %collective-permute-start.2 = (f32[1,392,128]{2,1,0:T(8,128)S(1)}, f32[1,392,128]{2,1,0:T(8,128)S(1)}, u32[]{:S(2)}, u32[]{:S(2)}) collective-permute-start(f32[1,392,128]{2,1,0:T(8,128)S(1)} %get-tuple-element.15.own_ref), channel_id=1, source_target_pairs={{0,4},{1,5},{2,6},{3,7},{4,0},{5,1},{6,2},{7,3},{8,12},{9,13},{10,... | collective-permute-start | bytes 602120 | tf_op jit(solution)/shard_map/ppermute | solution.py:377
  68.7 4.8 %collective-permute-done.2.other_ref = f32[1,392,128]{2,1,0:T(8,128)S(1)} collective-permute-done((f32[1,392,128]{2,1,0:T(8,128)S(1)}, f32[1,392,128]{2,1,0:T(8,128)S(1)}, u32[]{:S(2)}, u32[]{:S(2)}) %collective-permute-start.2) | collective-permute-done | bytes 200736 | tf_op jit(solution)/shard_map/ppermute | solution.py:377
  73.5 9.4 %shard_map.116 = (f32[136,128]{1,0:T(8,128)S(1)}, f32[2,392,128]{2,1,0:T(8,128)S(1)}) custom-call(s32[2]{0:T(128)S(1)} %pad_add_fusion.place_ref, f32[1,392,128]{2,1,0:T(8,128)S(1)} %get-tuple-element.15.own_ref, f32[1,392,128]{2,1,0:T(8,128)S(1)} %collective-permute-done.2.other_ref, f32[2,392,128]{2,1,0:T(8,128)S(1)} %get-tuple-element.16.sides_ref), custom_call_target="tpu_custom_call" | custom-call | tf_op jit(solution)/shard_map/pallas_call | solution.py:324
  82.9 2.3 %collective-permute-start.3 = (f32[136,128]{1,0:T(8,128)S(1)}, f32[136,128]{1,0:T(8,128)S(1)}, u32[]{:S(2)}, u32[]{:S(2)}) collective-permute-start(f32[136,128]{1,0:T(8,128)S(1)} %get-tuple-element.17), channel_id=1, source_target_pairs={{0,8},{1,9},{2,10},{3,11},{4,12},{5,13},{6,14},{7,15},{8,0},{9,1},... | collective-permute-start | bytes 208904 | tf_op jit(solution)/shard_map/ppermute | solution.py:377
  85.2 2.9 %collective-permute-done.3.other_ref = f32[136,128]{1,0:T(8,128)S(1)} collective-permute-done((f32[136,128]{1,0:T(8,128)S(1)}, f32[136,128]{1,0:T(8,128)S(1)}, u32[]{:S(2)}, u32[]{:S(2)}) %collective-permute-start.3) | collective-permute-done | bytes 69664 | tf_op jit(solution)/shard_map/ppermute | solution.py:377
  88.1 32.8 %shard_map.117 = (f32[4,128]{1,0:T(4,128)}, f32[4,128]{1,0:T(4,128)}, f32[4,128]{1,0:T(4,128)}) custom-call(s32[2]{0:T(128)S(1)} %pad_add_fusion.place_ref, f32[7,392,128]{2,1,0:T(8,128)S(1)} %get-tuple-element.11.locals_ref, f32[136,128]{1,0:T(8,128)S(1)} %collective-permute-done.3.other_ref, f32[2,392,128]{2,1,0:T(8,128)S(1)} %get-tuple-element.18.sides_ref), custom_call_target="tpu_custom_call" | custom-call | tf_op jit(solution)/shard_map/pallas_call | solution.py:324
  (12 shorter events, 0.2 us)
Async XLA Ops:
  0.6 18.0 %copy-start = (f32[128]{0:T(128)S(1)}, f32[128]{0:T(128)}, u32[]{:S(2)}) copy-start(f32[128]{0:T(128)} %param.15) | copy-start | bytes 1540
  0.6 18.0 %copy-start.1 = (f32[128]{0:T(128)S(1)}, f32[128]{0:T(128)}, u32[]{:S(2)}) copy-start(f32[128]{0:T(128)} %param.16) | copy-start | bytes 1540
  2.8 14.5 %all-to-all-start = ((f32[8,1,288]{2,1,0:T(1,128)}), f32[8,1,288]{2,1,0:T(1,128)S(1)}, u32[]{:S(2)}, u32[]{:S(2)}) async-start(f32[8,1,288]{2,1,0:T(1,128)} %reshape.60), calls=%async_computation | async-start | bytes 24576 | tf_op jit(solution)/shard_map/all_to_all | solution.py:357
  40.8 1.5 %collective-permute-start = (f32[1,392,128]{2,1,0:T(8,128)S(1)}, f32[1,392,128]{2,1,0:T(8,128)S(1)}, u32[]{:S(2)}, u32[]{:S(2)}) collective-permute-start(f32[1,392,128]{2,1,0:T(8,128)S(1)} %get-tuple-element.12.own_ref), channel_id=1, source_target_pairs={{0,1},{1,0},{2,3},{3,2},{4,5},{5,4},{6,7},{7,6},{8,9},{9,8},{10,11... | collective-permute-start | bytes 602120 | tf_op jit(solution)/shard_map/ppermute | solution.py:377
  50.2 7.3 %collective-permute-start.1 = (f32[1,392,128]{2,1,0:T(8,128)S(1)}, f32[1,392,128]{2,1,0:T(8,128)S(1)}, u32[]{:S(2)}, u32[]{:S(2)}) collective-permute-start(f32[1,392,128]{2,1,0:T(8,128)S(1)} %get-tuple-element.13.own_ref), channel_id=1, source_target_pairs={{0,2},{1,3},{2,0},{3,1},{4,6},{5,7},{6,4},{7,5},{8,10},{9,11},{10,... | collective-permute-start | bytes 602120 | tf_op jit(solution)/shard_map/ppermute | solution.py:377
  67.0 6.5 %collective-permute-start.2 = (f32[1,392,128]{2,1,0:T(8,128)S(1)}, f32[1,392,128]{2,1,0:T(8,128)S(1)}, u32[]{:S(2)}, u32[]{:S(2)}) collective-permute-start(f32[1,392,128]{2,1,0:T(8,128)S(1)} %get-tuple-element.15.own_ref), channel_id=1, source_target_pairs={{0,4},{1,5},{2,6},{3,7},{4,0},{5,1},{6,2},{7,3},{8,12},{9,13},{10,... | collective-permute-start | bytes 602120 | tf_op jit(solution)/shard_map/ppermute | solution.py:377
  82.9 5.2 %collective-permute-start.3 = (f32[136,128]{1,0:T(8,128)S(1)}, f32[136,128]{1,0:T(8,128)S(1)}, u32[]{:S(2)}, u32[]{:S(2)}) collective-permute-start(f32[136,128]{1,0:T(8,128)S(1)} %get-tuple-element.17), channel_id=1, source_target_pairs={{0,8},{1,9},{2,10},{3,11},{4,12},{5,13},{6,14},{7,15},{8,0},{9,1},... | collective-permute-start | bytes 208904 | tf_op jit(solution)/shard_map/ppermute | solution.py:377
